TPU v7x, 32 devices: a whole 2x2x4 slice. The times are simulated.
32 devices in a mesh: fsdp: 32 (over z, y, x, core).
Axes of the slice: x: 2, y: 2, z: 4, core: 2. Of those that a mesh axis runs over, the one named last changes fastest.
Arguments:
- tokens: float32 [160, 196, 512], P('fsdp'), may hold values from -6 to 6
- live_count: int32 [32], P('fsdp'), may hold values from 4 to 5, as said below
- rel_index: int32 [49, 49], replicated, may hold values from 0 to 175, as said below
- mask_ids: int32 [196], replicated, may hold values from 0 to 8, as said below
- norm1_gain: bfloat16 [2, 512], P(None, 'fsdp'), may hold values from 0.5 to 1.5
- norm1_bias: bfloat16 [2, 512], P(None, 'fsdp'), may hold values from -4 to 4
- qkv_weight: bfloat16 [2, 512, 1536], P(None, 'fsdp'), may hold values from -0.25 to 0.25
- qv_bias: bfloat16 [2, 1024], P(None, 'fsdp'), may hold values from -4 to 4
- bias_table: bfloat16 [2, 2816], P(None, 'fsdp'), may hold values from -4 to 4
- proj_weight: bfloat16 [2, 512, 512], P(None, 'fsdp'), may hold values from -1.5 to 1.5
- proj_bias: bfloat16 [2, 512], P(None, 'fsdp'), may hold values from -4 to 4
- norm2_gain: bfloat16 [2, 512], P(None, 'fsdp'), may hold values from 0.5 to 1.5
- norm2_bias: bfloat16 [2, 512], P(None, 'fsdp'), may hold values from -4 to 4
- fc1_weight: bfloat16 [2, 512, 2048], P(None, 'fsdp'), may hold values from -0.25 to 0.25
- fc1_bias: bfloat16 [2, 2048], P(None, 'fsdp'), may hold values from -4 to 4
- fc2_weight: bfloat16 [2, 2048, 512], P(None, 'fsdp'), may hold values from -0.125 to 0.125
- fc2_bias: bfloat16 [2, 512], P(None, 'fsdp'), may hold values from -4 to 4
- cotangent: float32 [160, 196, 512], P('fsdp'), may hold values from -6 to 6
Outputs:
- result: float32 [160, 196, 512], P('fsdp')
- tokens_grad: float32 [160, 196, 512], P('fsdp')
- norm1_gain_grad: float32 [2, 512], P(None, 'fsdp')
- norm1_bias_grad: float32 [2, 512], P(None, 'fsdp')
- qkv_weight_grad: float32 [2, 512, 1536], P(None, 'fsdp')
- qv_bias_grad: float32 [2, 1024], P(None, 'fsdp')
- bias_table_grad: float32 [2, 2816], P(None, 'fsdp')
- proj_weight_grad: float32 [2, 512, 512], P(None, 'fsdp')
- proj_bias_grad: float32 [2, 512], P(None, 'fsdp')
- norm2_gain_grad: float32 [2, 512], P(None, 'fsdp')
- norm2_bias_grad: float32 [2, 512], P(None, 'fsdp')
- fc1_weight_grad: float32 [2, 512, 2048], P(None, 'fsdp')
- fc1_bias_grad: float32 [2, 2048], P(None, 'fsdp')
- fc2_weight_grad: float32 [2, 2048, 512], P(None, 'fsdp')
- fc2_bias_grad: float32 [2, 512], P(None, 'fsdp')
Inputs may be any that keep to these rules, and one draw needn't show every extreme that they name: Device i holds live_count[i] live images in its first slots of tokens; the rest of its 5 slots are empty. Some device holds 5 live images and some 4. `rel_index`: query and key position pairs of a window with the same offset in rows and columns name the same row of the bias table, pairs with different offsets different rows; rows 0 and 175 are always named. `mask_ids`: positions of the rolled grid in one of the nine regions that the roll by 3 makes (three bands of rows times three bands of columns) share a label; different regions may share a label too; the first region is labelled 0 and the last 8.
All inputs are finite; a program needn't handle non-finite values.
Results may differ from a plain program's by a relative error of at most 0.015.
Values may be sent and summed in bfloat16 or wider, within the bound.
A program may use at most 256 MiB of HBM per device.

v0:
```python
import jax
import jax.numpy as jnp
from jax import lax
from jax.sharding import PartitionSpec as P

HEAD = 32
WIN = 7
GRID = 14
TABLE = 176
LAYERS = 2
HEADS = 16
SHIFT = 3


norm_eps = 1e-05
mask_fill = -100.0


def to_windows(grid_rows):
    images = grid_rows.shape[0]
    features = grid_rows.shape[-1]
    split = grid_rows.reshape(images, GRID // WIN, WIN, GRID // WIN, WIN, features)
    split = split.transpose(0, 1, 3, 2, 4, 5)
    return split.reshape(images * (GRID // WIN) ** 2, WIN * WIN, features)


def from_windows(windows, images):
    features = windows.shape[-1]
    split = windows.reshape(images, GRID // WIN, GRID // WIN, WIN, WIN, features)
    split = split.transpose(0, 1, 3, 2, 4, 5)
    return split.reshape(images, GRID, GRID, features)


def enter_windows(token_rows, shifted):
    images = token_rows.shape[0]
    grid_rows = token_rows.reshape(images, GRID, GRID, token_rows.shape[-1])
    if shifted:
        grid_rows = jnp.roll(grid_rows, (-SHIFT, -SHIFT), axis=(1, 2))
    return to_windows(grid_rows)


def leave_windows(windows, images, shifted):
    grid_rows = from_windows(windows, images)
    if shifted:
        grid_rows = jnp.roll(grid_rows, (SHIFT, SHIFT), axis=(1, 2))
    return grid_rows.reshape(images, GRID * GRID, windows.shape[-1])


def layer_norm(stream, gain_row, offset):
    average = jnp.mean(stream, axis=-1, keepdims=True)
    centred = stream - average
    variance = jnp.mean(centred * centred, axis=-1, keepdims=True)
    return centred * lax.rsqrt(variance + norm_eps) * gain_row + offset


def gelu_exact(hidden):
    return jax.nn.gelu(hidden, approximate=False)


def contract_rows(rows_left, rows_right, precision=None):
    return lax.dot_general(
        rows_left,
        rows_right,
        (((0,), (0,)), ((), ())),
        precision=precision,
        preferred_element_type=jnp.float32,
    )


def times_transposed(rows_left, rows_right):
    return lax.dot_general(
        rows_left, rows_right, (((1,), (1,)), ((), ())), preferred_element_type=jnp.float32
    )


def position_bias(table_flat, rel_onehot):
    table_rows = table_flat.astype(jnp.float32).reshape(TABLE, HEADS)
    lookup = jnp.dot(
        rel_onehot, table_rows, precision=lax.Precision.HIGHEST, preferred_element_type=jnp.float32
    )
    return lookup.reshape(WIN * WIN, WIN * WIN, HEADS).transpose(2, 0, 1)


def attend_scores(queries, keys_low, bias_heads, mask_add):
    scores = jnp.einsum("wqhc,wkhc->whqk", queries, keys_low, preferred_element_type=jnp.float32)
    scores = scores + bias_heads[None]
    if mask_add is not None:
        window_count = scores.shape[0]
        per_image = mask_add.shape[0]
        scores = (
            scores.reshape(window_count // per_image, per_image, HEADS, WIN * WIN, WIN * WIN)
            + mask_add[None, :, None]
        ).reshape(scores.shape)
    return scores


def layer_forward(stream, weights, shifted, rel_onehot, mask_add):
    (
        gain_one,
        offset_one,
        qkv_w,
        qv_b,
        table_flat,
        proj_w,
        proj_b,
        gain_two,
        offset_two,
        up_w,
        up_b,
        down_w,
        down_b,
    ) = weights
    images = stream.shape[0]
    features = stream.shape[-1]
    normed_one = layer_norm(
        stream, gain_one.astype(jnp.float32), offset_one.astype(jnp.float32)
    ).astype(jnp.bfloat16)
    windows = enter_windows(normed_one, shifted).reshape(-1, features)
    window_count = windows.shape[0] // (WIN * WIN)
    qv_float = qv_b.astype(jnp.float32)
    qkv = jnp.dot(windows, qkv_w, preferred_element_type=jnp.float32)
    qkv = qkv + jnp.concatenate(
        [qv_float[:features], jnp.zeros((features,), jnp.float32), qv_float[features:]]
    )
    head_shape = (window_count, WIN * WIN, HEADS, HEAD)
    head_scale = HEAD ** (-0.5)
    queries = (qkv[:, :features] * head_scale).astype(jnp.bfloat16).reshape(head_shape)
    keys_low = qkv[:, features : 2 * features].astype(jnp.bfloat16).reshape(head_shape)
    values_low = qkv[:, 2 * features :].astype(jnp.bfloat16).reshape(head_shape)
    scores = attend_scores(queries, keys_low, position_bias(table_flat, rel_onehot), mask_add)
    row_top = jnp.max(scores, axis=-1, keepdims=True)
    log_total = row_top + jnp.log(jnp.sum(jnp.exp(scores - row_top), axis=-1, keepdims=True))
    probs_low = jnp.exp(scores - log_total).astype(jnp.bfloat16)
    attended = jnp.einsum(
        "whqk,wkhc->wqhc", probs_low, values_low, preferred_element_type=jnp.float32
    )
    attended = attended.astype(jnp.bfloat16).reshape(-1, features)
    projected = jnp.dot(attended, proj_w, preferred_element_type=jnp.float32) + proj_b.astype(
        jnp.float32
    )
    stream_mid = stream + leave_windows(
        projected.reshape(window_count, WIN * WIN, features), images, shifted
    )
    normed_two = layer_norm(
        stream_mid, gain_two.astype(jnp.float32), offset_two.astype(jnp.float32)
    ).astype(jnp.bfloat16)
    hidden_pre = jnp.dot(
        normed_two.reshape(-1, features), up_w, preferred_element_type=jnp.float32
    ) + up_b.astype(jnp.float32)
    activ_low = gelu_exact(hidden_pre).astype(jnp.bfloat16)
    branch_out = jnp.dot(activ_low, down_w, preferred_element_type=jnp.float32) + down_b.astype(
        jnp.float32
    )
    output = stream_mid + branch_out.reshape(stream.shape)
    saved_state = (
        stream,
        windows,
        queries,
        keys_low,
        values_low,
        log_total,
        attended,
        stream_mid,
        normed_two,
        hidden_pre,
        activ_low,
    )
    return (output, saved_state)


def layer_backward(grad_out, saved_state, weights, shifted, rel_onehot, mask_add):
    (
        gain_one,
        offset_one,
        qkv_w,
        qv_b,
        table_flat,
        proj_w,
        proj_b,
        gain_two,
        offset_two,
        up_w,
        up_b,
        down_w,
        down_b,
    ) = weights
    (
        stream,
        windows,
        queries,
        keys_low,
        values_low,
        log_total,
        attended,
        stream_mid,
        normed_two,
        hidden_pre,
        activ_low,
    ) = saved_state
    images = stream.shape[0]
    features = stream.shape[-1]
    window_count = windows.shape[0] // (WIN * WIN)
    grad_rows = grad_out.reshape(-1, features)
    grad_down_b = jnp.sum(grad_rows, axis=0)
    grad_low = grad_rows.astype(jnp.bfloat16)
    grad_down_w = contract_rows(activ_low, grad_low)
    grad_activ = times_transposed(grad_low, down_w)
    gelu_pull = jax.vjp(gelu_exact, hidden_pre)[1]
    grad_hidden = gelu_pull(grad_activ)[0]
    grad_up_b = jnp.sum(grad_hidden, axis=0)
    grad_hidden_low = grad_hidden.astype(jnp.bfloat16)
    grad_up_w = contract_rows(normed_two.reshape(-1, features), grad_hidden_low)
    grad_normed_two = times_transposed(grad_hidden_low, up_w).reshape(stream.shape)
    norm_pull = jax.vjp(
        layer_norm, stream_mid, gain_two.astype(jnp.float32), offset_two.astype(jnp.float32)
    )[1]
    part_mid, grad_gain_two, grad_offset_two = norm_pull(grad_normed_two)
    grad_mid = grad_out + part_mid
    grad_proj = enter_windows(grad_mid, shifted).reshape(-1, features)
    grad_proj_b = jnp.sum(grad_proj, axis=0)
    grad_proj_low = grad_proj.astype(jnp.bfloat16)
    grad_proj_w = contract_rows(attended, grad_proj_low)
    head_shape = (window_count, WIN * WIN, HEADS, HEAD)
    grad_attended = times_transposed(grad_proj_low, proj_w).astype(jnp.bfloat16).reshape(head_shape)
    scores = attend_scores(queries, keys_low, position_bias(table_flat, rel_onehot), mask_add)
    attn_probs = jnp.exp(scores - log_total)
    probs_low = attn_probs.astype(jnp.bfloat16)
    grad_values = jnp.einsum(
        "whqk,wqhc->wkhc", probs_low, grad_attended, preferred_element_type=jnp.float32
    )
    grad_probs = jnp.einsum(
        "wqhc,wkhc->whqk", grad_attended, values_low, preferred_element_type=jnp.float32
    )
    grad_scores = attn_probs * (
        grad_probs - jnp.sum(grad_probs * attn_probs, axis=-1, keepdims=True)
    )
    bias_sum = jnp.sum(grad_scores, axis=0).transpose(1, 2, 0).reshape(WIN * WIN * WIN * WIN, HEADS)
    grad_table = contract_rows(rel_onehot, bias_sum, lax.Precision.HIGHEST).reshape(-1)
    grad_scores_low = grad_scores.astype(jnp.bfloat16)
    head_scale = HEAD ** (-0.5)
    grad_queries = (
        jnp.einsum("whqk,wkhc->wqhc", grad_scores_low, keys_low, preferred_element_type=jnp.float32)
        * head_scale
    )
    grad_keys = jnp.einsum(
        "whqk,wqhc->wkhc", grad_scores_low, queries, preferred_element_type=jnp.float32
    )
    grad_qkv = jnp.concatenate(
        [
            grad_queries.reshape(-1, features),
            grad_keys.reshape(-1, features),
            grad_values.reshape(-1, features),
        ],
        axis=1,
    )
    grad_qv_b = jnp.concatenate(
        [jnp.sum(grad_qkv[:, :features], axis=0), jnp.sum(grad_qkv[:, 2 * features :], axis=0)]
    )
    grad_qkv_low = grad_qkv.astype(jnp.bfloat16)
    grad_qkv_w = contract_rows(windows, grad_qkv_low)
    grad_normed_one = leave_windows(
        times_transposed(grad_qkv_low, qkv_w).reshape(window_count, WIN * WIN, features),
        images,
        shifted,
    )
    norm_pull = jax.vjp(
        layer_norm, stream, gain_one.astype(jnp.float32), offset_one.astype(jnp.float32)
    )[1]
    part_in, grad_gain_one, grad_offset_one = norm_pull(grad_normed_one)
    grad_in = grad_mid + part_in
    return (
        grad_in,
        (
            grad_gain_one,
            grad_offset_one,
            grad_qkv_w,
            grad_qv_b,
            grad_table,
            grad_proj_w,
            grad_proj_b,
            grad_gain_two,
            grad_offset_two,
            grad_up_w,
            grad_up_b,
            grad_down_w,
            grad_down_b,
        ),
    )


def stack_member(layer_grads, member):
    return jnp.stack([grads_layer[member] for grads_layer in layer_grads])


def shards(
    tokens,
    live_count,
    rel_index,
    mask_ids,
    norm1_gain,
    norm1_bias,
    qkv_weight,
    qv_bias,
    bias_table,
    proj_weight,
    proj_bias,
    norm2_gain,
    norm2_bias,
    fc1_weight,
    fc1_bias,
    fc2_weight,
    fc2_bias,
    cotangent,
):
    images = tokens.shape[0]
    live_rows = (jnp.arange(images) < live_count[0]).astype(jnp.float32)[:, None, None]
    rel_onehot = (rel_index.reshape(-1)[:, None] == jnp.arange(TABLE)[None, :]).astype(jnp.float32)
    region = to_windows(mask_ids.reshape(1, GRID, GRID, 1)).reshape(-1, WIN * WIN)
    mask_add = jnp.where(region[:, :, None] == region[:, None, :], 0.0, mask_fill).astype(
        jnp.float32
    )
    stream = tokens
    saved_all = []
    gathered_all = []
    for layer_index in range(LAYERS):
        weights = (
            lax.all_gather(norm1_gain[layer_index], "fsdp", axis=0, tiled=True),
            lax.all_gather(norm1_bias[layer_index], "fsdp", axis=0, tiled=True),
            lax.all_gather(qkv_weight[layer_index], "fsdp", axis=0, tiled=True),
            lax.all_gather(qv_bias[layer_index], "fsdp", axis=0, tiled=True),
            lax.all_gather(bias_table[layer_index], "fsdp", axis=0, tiled=True),
            lax.all_gather(proj_weight[layer_index], "fsdp", axis=0, tiled=True),
            lax.all_gather(proj_bias[layer_index], "fsdp", axis=0, tiled=True),
            lax.all_gather(norm2_gain[layer_index], "fsdp", axis=0, tiled=True),
            lax.all_gather(norm2_bias[layer_index], "fsdp", axis=0, tiled=True),
            lax.all_gather(fc1_weight[layer_index], "fsdp", axis=0, tiled=True),
            lax.all_gather(fc1_bias[layer_index], "fsdp", axis=0, tiled=True),
            lax.all_gather(fc2_weight[layer_index], "fsdp", axis=0, tiled=True),
            lax.all_gather(fc2_bias[layer_index], "fsdp", axis=0, tiled=True),
        )
        shifted = layer_index % 2 == 1
        stream, saved_state = layer_forward(
            stream, weights, shifted, rel_onehot, mask_add if shifted else None
        )
        saved_all.append(saved_state)
        gathered_all.append(weights)
    result = stream * live_rows
    grad_stream = cotangent * live_rows
    layer_grads = [None] * LAYERS
    for layer_index in range(LAYERS - 1, -1, -1):
        shifted = layer_index % 2 == 1
        weights = (
            lax.all_gather(norm1_gain[layer_index], "fsdp", axis=0, tiled=True),
            lax.all_gather(norm1_bias[layer_index], "fsdp", axis=0, tiled=True),
            lax.all_gather(qkv_weight[layer_index], "fsdp", axis=0, tiled=True),
            lax.all_gather(qv_bias[layer_index], "fsdp", axis=0, tiled=True),
            lax.all_gather(bias_table[layer_index], "fsdp", axis=0, tiled=True),
            lax.all_gather(proj_weight[layer_index], "fsdp", axis=0, tiled=True),
            lax.all_gather(proj_bias[layer_index], "fsdp", axis=0, tiled=True),
            lax.all_gather(norm2_gain[layer_index], "fsdp", axis=0, tiled=True),
            lax.all_gather(norm2_bias[layer_index], "fsdp", axis=0, tiled=True),
            lax.all_gather(fc1_weight[layer_index], "fsdp", axis=0, tiled=True),
            lax.all_gather(fc1_bias[layer_index], "fsdp", axis=0, tiled=True),
            lax.all_gather(fc2_weight[layer_index], "fsdp", axis=0, tiled=True),
            lax.all_gather(fc2_bias[layer_index], "fsdp", axis=0, tiled=True),
        )
        grad_stream, full_grads = layer_backward(
            grad_stream,
            saved_all[layer_index],
            weights,
            shifted,
            rel_onehot,
            mask_add if shifted else None,
        )
        layer_grads[layer_index] = (
            lax.psum_scatter(full_grads[0], "fsdp", scatter_dimension=0, tiled=True),
            lax.psum_scatter(full_grads[1], "fsdp", scatter_dimension=0, tiled=True),
            lax.psum_scatter(full_grads[2], "fsdp", scatter_dimension=0, tiled=True),
            lax.psum_scatter(full_grads[3], "fsdp", scatter_dimension=0, tiled=True),
            lax.psum_scatter(full_grads[4], "fsdp", scatter_dimension=0, tiled=True),
            lax.psum_scatter(full_grads[5], "fsdp", scatter_dimension=0, tiled=True),
            lax.psum_scatter(full_grads[6], "fsdp", scatter_dimension=0, tiled=True),
            lax.psum_scatter(full_grads[7], "fsdp", scatter_dimension=0, tiled=True),
            lax.psum_scatter(full_grads[8], "fsdp", scatter_dimension=0, tiled=True),
            lax.psum_scatter(full_grads[9], "fsdp", scatter_dimension=0, tiled=True),
            lax.psum_scatter(full_grads[10], "fsdp", scatter_dimension=0, tiled=True),
            lax.psum_scatter(full_grads[11], "fsdp", scatter_dimension=0, tiled=True),
            lax.psum_scatter(full_grads[12], "fsdp", scatter_dimension=0, tiled=True),
        )
    finished = tuple((stack_member(layer_grads, member) for member in range(13)))
    return (result, grad_stream) + tuple(finished)


def solution(mesh):
    in_specs = (
        P("fsdp", None, None),
        P("fsdp"),
        P(),
        P(),
        P(None, "fsdp"),
        P(None, "fsdp"),
        P(None, "fsdp", None),
        P(None, "fsdp"),
        P(None, "fsdp"),
        P(None, "fsdp", None),
        P(None, "fsdp"),
        P(None, "fsdp"),
        P(None, "fsdp"),
        P(None, "fsdp", None),
        P(None, "fsdp"),
        P(None, "fsdp", None),
        P(None, "fsdp"),
        P("fsdp", None, None),
    )
    out_specs = (
        P("fsdp", None, None),
        P("fsdp", None, None),
        P(None, "fsdp"),
        P(None, "fsdp"),
        P(None, "fsdp", None),
        P(None, "fsdp"),
        P(None, "fsdp"),
        P(None, "fsdp", None),
        P(None, "fsdp"),
        P(None, "fsdp"),
        P(None, "fsdp"),
        P(None, "fsdp", None),
        P(None, "fsdp"),
        P(None, "fsdp", None),
        P(None, "fsdp"),
    )
    return jax.shard_map(shards, mesh=mesh, in_specs=in_specs, out_specs=out_specs, check_vma=False)
```

profile of v0, /device:TPU:0, one launch (start us, length us, event | category | flops | bytes accessed | tf_op | source)
XLA Modules:
  0.0 1870.7 jit_solution(18304563424900848513)
XLA Ops:
  25.1 42.9 %all-reduce.37 = (bf16[512]{0:T(512)(128)(2,1)S(1)}, bf16[512]{0:T(512)(128)(2,1)S(1)}, bf16[1024]{0:T(1024)(128)(2,1)S(1)}, bf16[2816]{0:T(1024)(128)(2,1)S(1)}...) all-reduce(bf16[512]{0:T(512)(128)(2,1)S(1)} %dynamic-update-slice., ...), channel_id=3, replica_groups=mesh['fsdp'=32] {'fsdp'}, use_global_device_ids=true, to_apply=%add.1 | all-reduce | flops 17920 | bytes 71680
  80.4 45.1 %all-gather.5 = bf16[1,512,512]{2,1,0:T(8,128)(2,1)} all-gather(bf16[1,16,512]{2,1,0:T(8,128)(2,1)S(1)} %get-tuple-element.99), channel_id=7, replica_groups=mesh['fsdp'=32] {'fsdp'}, dimensions={1}, use_global_device_ids=true | all-gather | bytes 540672 | tf_op jit(solution)/shard_map/all_gather | solution.py:332
  129.0 41.1 %all-gather.18 = bf16[1,512,512]{2,1,0:T(8,128)(2,1)} all-gather(bf16[1,16,512]{2,1,0:T(8,128)(2,1)S(1)} %get-tuple-element.98), channel_id=20, replica_groups=mesh['fsdp'=32] {'fsdp'}, dimensions={1}, use_global_device_ids=true | all-gather | bytes 540672 | tf_op jit(solution)/shard_map/all_gather | solution.py:332
  217.5 7.0 copy.121
  260.2 22.8 %multiply_convert_fusion.1 = (bf16[980,2048]{1,0:T(8,128)(2,1)}, f32[980,2048]{1,0:T(8,128)}, f32[980,2048]{1,0:T(8,128)}) fusion(f32[2048]{0:T(1024)S(1)} %convert_element_type.245, bf16[980,512]{1,0:T(8,128)(2,1)S(1)} %reshape.377, bf16[1,512,2048]{2,1,0:T(8,128)(2,1)} %all-gather.35.cloned.1.call-done), kind=kOutput, calls=%fused_computation.29 | convolution fusion | flops 2187673600 | bytes 23179264 | tf_op jit(solution)/shard_map/dot_general | solution.py:147
  332.0 7.0 copy.133
  379.8 22.8 %multiply_convert_fusion = (bf16[980,2048]{1,0:T(8,128)(2,1)}, f32[980,2048]{1,0:T(8,128)}, f32[980,2048]{1,0:T(8,128)}) fusion(f32[2048]{0:T(1024)S(1)} %copy-done.83, bf16[980,512]{1,0:T(8,128)(2,1)S(1)} %reshape.388, bf16[1,512,2048]{2,1,0:T(8,128)(2,1)} %all-gather.41.cloned.1.call-done), kind=kOutput, calls=%fused_computation.16 | convolution fusion | flops 2187673600 | bytes 23179264 | tf_op jit(solution)/shard_map/dot_general | solution.py:147
  402.6 9.6 fusion.125
  459.2 12.4 multiply_reduce_fusion.1
  471.7 6.9 fusion.105
  487.2 7.5 bitcast_convert_fusion.2
  542.4 10.2 fusion.126
  573.8 6.7 copy.157
  580.6 11.4 multiply_reduce_fusion
  592.0 7.1 fusion.104
  728.4 93.3 %all-reduce.40.cloned.1.call-done = (f32[512]{0:T(512)}, f32[512]{0:T(512)}, f32[512]{0:T(512)}, f32[512]{0:T(512)}, f32[1024]{0:T(1024)}, /*index=5*/f32[1024]{...) async-done(((f32[512]{0:T(512)}, f32[512]{0:T(512)}, ...) | async-done | bytes 71696
  833.6 127.8 %reduce-scatter.15.cloned.1.call-done = f32[16,512]{1,0:T(8,128)} async-done(((f32[512,512]{1,0:T(8,128)}), f32[16,512]{1,0:T(8,128)}) %reduce-scatter.15.cloned.1.call-update) | async-done | bytes 32784 | tf_op jit(solution)/shard_map/reduce_scatter | solution.py:381
  961.4 133.1 %reduce-scatter.13.cloned.1.call-done = f32[16,512]{1,0:T(8,128)} async-done(((f32[512,512]{1,0:T(8,128)}), f32[16,512]{1,0:T(8,128)}) %reduce-scatter.13.cloned.1.call-update) | async-done | bytes 32784 | tf_op jit(solution)/shard_map/reduce_scatter | solution.py:381
  1095.9 101.4 %reduce-scatter.11.cloned.1.call-done = f32[16,1536]{1,0:T(8,128)} async-done(((f32[512,1536]{1,0:T(8,128)}), f32[16,1536]{1,0:T(8,128)}) %reduce-scatter.11.cloned.1.call-update) | async-done | bytes 98320 | tf_op jit(solution)/shard_map/reduce_scatter | solution.py:378
  1197.2 105.9 %reduce-scatter.9.cloned.1.call-done = f32[16,1536]{1,0:T(8,128)} async-done(((f32[512,1536]{1,0:T(8,128)}), f32[16,1536]{1,0:T(8,128)}) %reduce-scatter.9.cloned.1.call-update) | async-done | bytes 98320 | tf_op jit(solution)/shard_map/reduce_scatter | solution.py:378
  1304.8 140.5 %reduce-scatter.19.cloned.1.call-done = f32[16,2048]{1,0:T(8,128)} async-done(((f32[512,2048]{1,0:T(8,128)}), f32[16,2048]{1,0:T(8,128)}) %reduce-scatter.19.cloned.1.call-update) | async-done | bytes 131088 | tf_op jit(solution)/shard_map/reduce_scatter | solution.py:385
  1445.3 139.1 %reduce-scatter.17.cloned.1.call-done = f32[16,2048]{1,0:T(8,128)} async-done(((f32[512,2048]{1,0:T(8,128)}), f32[16,2048]{1,0:T(8,128)}) %reduce-scatter.17.cloned.1.call-update) | async-done | bytes 131088 | tf_op jit(solution)/shard_map/reduce_scatter | solution.py:385
  1586.0 137.2 %reduce-scatter.23.cloned.1.call-done = f32[64,512]{1,0:T(8,128)} async-done(((f32[2048,512]{1,0:T(8,128)}), f32[64,512]{1,0:T(8,128)}) %reduce-scatter.23.cloned.1.call-update) | async-done | bytes 131088 | tf_op jit(solution)/shard_map/reduce_scatter | solution.py:387
  1723.3 139.0 %reduce-scatter.21.cloned.1.call-done = f32[64,512]{1,0:T(8,128)} async-done(((f32[2048,512]{1,0:T(8,128)}), f32[64,512]{1,0:T(8,128)}) %reduce-scatter.21.cloned.1.call-update) | async-done | bytes 131088 | tf_op jit(solution)/shard_map/reduce_scatter | solution.py:387
  (532 shorter events, 476.6 us)
Async XLA Ops:
  7.2 63.3 %copy-start.2 = (f32[5,196,512]{2,1,0:T(8,128)S(1)}, f32[5,196,512]{2,1,0:T(8,128)}, u32[]{:S(2)}) copy-start(f32[5,196,512]{2,1,0:T(8,128)} %param.18) | copy-start | bytes 6021124
  7.2 169.9 %all-gather.33.cloned.1.call-start = ((), (), s32[]{:S(2)}) async-start(), calls=%async_computation.16 | async-start | bytes 1622016 | tf_op jit(solution)/shard_map/all_gather | solution.py:329
  8.9 251.4 %all-gather.35.cloned.1.call-start = ((), (), s32[]{:S(2)}) async-start(), calls=%async_computation.17 | async-start | bytes 2162688 | tf_op jit(solution)/shard_map/all_gather | solution.py:336
  10.5 272.6 %all-gather.37.cloned.1.call-start = ((), (), s32[]{:S(2)}) async-start(), calls=%async_computation.18 | async-start | bytes 2162688 | tf_op jit(solution)/shard_map/all_gather | solution.py:338
  12.1 286.0 %all-gather.39.cloned.1.call-start = ((), (), s32[]{:S(2)}) async-start(), calls=%async_computation.19 | async-start | bytes 1622016 | tf_op jit(solution)/shard_map/all_gather | solution.py:329
  12.6 367.1 %all-gather.41.cloned.1.call-start = ((), (), s32[]{:S(2)}) async-start(), calls=%async_computation.20 | async-start | bytes 2162688 | tf_op jit(solution)/shard_map/all_gather | solution.py:336
  13.2 389.3 %all-gather.43.cloned.1.call-start = ((), (), s32[]{:S(2)}) async-start(), calls=%async_computation.21 | async-start | bytes 2162688 | tf_op jit(solution)/shard_map/all_gather | solution.py:338
  13.8 807.9 %all-reduce.40.cloned.1.call-start = ((), (), s32[]{:S(2)}) async-start(), calls=%async_computation.22 | async-start | bytes 147456
  14.5 156.7 %copy-start.84 = (f32[5]{0:T(128)}, f32[5]{0:T(128)S(1)}, u32[]{:S(2)}) copy-start(f32[5]{0:T(128)S(1)} %compare_convert_fusion) | copy-start | bytes 64
  75.0 50.6 %copy-start.87 = (s32[196]{0:T(256)S(1)}, s32[196]{0:T(256)}, u32[]{:S(2)}) copy-start(s32[196]{0:T(256)} %param.21) | copy-start | bytes 2356
  80.4 152.3 %copy-start.24 = (f32[16,49,49]{1,2,0:T(8,128)}, f32[16,49,49]{1,2,0:T(8,128)S(1)}, u32[]{:S(2)}) copy-start(f32[16,49,49]{1,2,0:T(8,128)S(1)} %copy.123) | copy-start | bytes 460996
  125.6 134.7 %copy-start.81 = (f32[2048]{0:T(1024)}, f32[2048]{0:T(1024)S(1)}, u32[]{:S(2)}) copy-start(f32[2048]{0:T(1024)S(1)} %convert_element_type.245) | copy-start | bytes 24580
  125.6 133.3 %copy-start.72 = (f32[512]{0:T(512)}, f32[512]{0:T(512)S(1)}, u32[]{:S(2)}) copy-start(f32[512]{0:T(512)S(1)} %convert_element_type.243) | copy-start | bytes 6148
  125.6 169.2 %copy-start.74 = (f32[512]{0:T(512)}, f32[512]{0:T(512)S(1)}, u32[]{:S(2)}) copy-start(f32[512]{0:T(512)S(1)} %convert_element_type.247) | copy-start | bytes 6148
  258.8 24.2 %copy-start.66 = (f32[5,196]{1,0:T(8,128)}, f32[5,196]{1,0:T(8,128)S(1)}, u32[]{:S(2)}) copy-start(f32[5,196]{1,0:T(8,128)S(1)} %multiply_reduce_fusion.12) | copy-start | bytes 11764
  259.6 23.4 %copy-start.60 = (f32[5,196]{1,0:T(8,128)}, f32[5,196]{1,0:T(8,128)S(1)}, u32[]{:S(2)}) copy-start(f32[5,196]{1,0:T(8,128)S(1)} %fusion.93) | copy-start | bytes 11764
  675.2 286.2 %reduce-scatter.15.cloned.1.call-start = ((), (), s32[]{:S(2)}) async-start(), calls=%async_computation.11 | async-start | bytes 1081344 | tf_op jit(solution)/shard_map/reduce_scatter | solution.py:381
  678.5 416.0 %reduce-scatter.13.cloned.1.call-start = ((), (), s32[]{:S(2)}) async-start(), calls=%async_computation.10 | async-start | bytes 1081344 | tf_op jit(solution)/shard_map/reduce_scatter | solution.py:381
  681.4 515.8 %reduce-scatter.11.cloned.1.call-start = ((), (), s32[]{:S(2)}) async-start(), calls=%async_computation.9 | async-start | bytes 3244032 | tf_op jit(solution)/shard_map/reduce_scatter | solution.py:378
  687.2 616.0 %reduce-scatter.9.cloned.1.call-start = ((), (), s32[]{:S(2)}) async-start(), calls=%async_computation.8 | async-start | bytes 3244032 | tf_op jit(solution)/shard_map/reduce_scatter | solution.py:378
  693.9 751.4 %reduce-scatter.19.cloned.1.call-start = ((), (), s32[]{:S(2)}) async-start(), calls=%async_computation.13 | async-start | bytes 4325376 | tf_op jit(solution)/shard_map/reduce_scatter | solution.py:385
  701.6 882.8 %reduce-scatter.17.cloned.1.call-start = ((), (), s32[]{:S(2)}) async-start(), calls=%async_computation.12 | async-start | bytes 4325376 | tf_op jit(solution)/shard_map/reduce_scatter | solution.py:385
  709.3 1013.9 %reduce-scatter.23.cloned.1.call-start = ((), (), s32[]{:S(2)}) async-start(), calls=%async_computation.15 | async-start | bytes 4325376 | tf_op jit(solution)/shard_map/reduce_scatter | solution.py:387
  717.2 1145.1 %reduce-scatter.21.cloned.1.call-start = ((), (), s32[]{:S(2)}) async-start(), calls=%async_computation.14 | async-start | bytes 4325376 | tf_op jit(solution)/shard_map/reduce_scatter | solution.py:387
  (93 other events, 449.0 us)
Sparse Core Ops, SparseCore 0:
  11.5 57.8 all-gather.32
  72.8 55.6 all-gather.34
  131.3 55.5 all-gather.36
  189.6 53.8 all-gather.38
  246.8 55.2 all-gather.40
  305.3 55.2 all-gather.42
  675.3 146.3 all-reduce.39
  823.9 137.3 reduce-scatter.14
  963.7 130.6 reduce-scatter.12
  1099.7 97.4 reduce-scatter.10
  1202.7 100.4 reduce-scatter.8
  1305.3 139.9 reduce-scatter.18
  1447.6 136.7 reduce-scatter.16
  1586.5 136.7 reduce-scatter.22
  1725.4 136.8 reduce-scatter.20
where the time goes:
time: 1880 us; the launch traced here: 1870 us
  waiting for transfers between devices  1120 us (60%)
  local copies, waits for them, and re-layouts  269 us (14%)
  matrix products  235 us (12%)
  blocking collectives  129 us (7%)
  other arithmetic  101 us (5%)
    reduce_scatter x2, waiting for transfers between devices, shards(): lax.psum_scatter(full_grads[9], 'fsdp', scatter_dimension=0, tiled=True)  280 us
    reduce_scatter x2, waiting for transfers between devices, shards(): lax.psum_scatter(full_grads[11], 'fsdp', scatter_dimension=0, tiled=True)  276 us
    reduce_scatter x2, waiting for transfers between devices, shards(): lax.psum_scatter(full_grads[5], 'fsdp', scatter_dimension=0, tiled=True)  261 us
    reduce_scatter x2, waiting for transfers between devices, shards(): lax.psum_scatter(full_grads[2], 'fsdp', scatter_dimension=0, tiled=True)  207 us
    unnamed x16, waiting for transfers between devices  95.1 us
    all_gather x2, blocking collectives, shards(): lax.all_gather(proj_weight[layer_index], 'fsdp', axis=0, tiled=True)  86.2 us
    dot_general x10, matrix products, contract_rows(): lax.dot_general(rows_left, rows_right, (((0,), (0,)), ((), ())), precisio...  47.2 us
    dot_general x2, matrix products, layer_forward(): jnp.dot(normed_two.reshape(-1, features), up_w, preferred_element_type=jn...  45.5 us
  transfers between devices with their start and end apart: 15, of which 9 were waited for; matrix products, arithmetic and copies ran while one was open for 17% of the time, Pallas kernels for 0%

commit v1 on v0

--- a/solution.py
+++ b/solution.py
@@ -1,3 +1,5 @@
+import functools
+
 import jax
 import jax.numpy as jnp
 from jax import lax
@@ -288,30 +290,65 @@
     )
 
 
-def stack_member(layer_grads, member):
-    return jnp.stack([grads_layer[member] for grads_layer in layer_grads])
+def bit_order(device_bits, turn):
+    order = list(range(device_bits))
+    if turn == 1 and device_bits > 2:
+        order[1], order[2] = order[2], order[1]
+    if turn == 2 and device_bits > 3:
+        order[1:4] = [order[3], order[1], order[2]]
+    return order
+
+
+def partner_pairs(devices, bit):
+    return [(place, place ^ (1 << bit)) for place in range(devices)]
+
+
+def my_bit(bit):
+    return (lax.axis_index("fsdp") >> bit) & 1
+
+
+def gather_blocks(block, devices, turn):
+    device_bits = devices.bit_length() - 1
+    held = []
+    for bit in reversed(bit_order(device_bits, turn)):
+        other = lax.ppermute(block, "fsdp", partner_pairs(devices, bit))
+        place = sum(1 for done in held if done > bit)
+        held.append(bit)
+        mine = my_bit(bit) == 0
+        block = jnp.stack(
+            [jnp.where(mine, block, other), jnp.where(mine, other, block)], axis=place
+        )
+    return block.reshape((devices,) + block.shape[device_bits:])
+
+
+def scatter_sums(blocks, devices, turn, wire):
+    device_bits = devices.bit_length() - 1
+    rest = blocks.shape[1:]
+    total = blocks.reshape((2,) * device_bits + rest)
+    left = list(range(device_bits - 1, -1, -1))
+    for bit in bit_order(device_bits, turn):
+        axis = left.index(bit)
+        left.remove(bit)
+        mine = my_bit(bit)
+        away = lax.dynamic_index_in_dim(total, 1 - mine, axis, keepdims=False).astype(wire)
+        kept = lax.dynamic_index_in_dim(total, mine, axis, keepdims=False)
+        arrived = lax.ppermute(away, "fsdp", partner_pairs(devices, bit))
+        total = kept.astype(jnp.float32) + arrived.astype(jnp.float32)
+        if left:
+            total = total.astype(wire)
+    return total
 
 
 def shards(
+    devices,
     tokens,
     live_count,
     rel_index,
     mask_ids,
-    norm1_gain,
-    norm1_bias,
-    qkv_weight,
-    qv_bias,
-    bias_table,
-    proj_weight,
-    proj_bias,
-    norm2_gain,
-    norm2_bias,
-    fc1_weight,
-    fc1_bias,
-    fc2_weight,
-    fc2_bias,
-    cotangent,
+    *params_and_cotangent,
 ):
+    params = params_and_cotangent[:13]
+    cotangent = params_and_cotangent[13]
     images = tokens.shape[0]
     live_rows = (jnp.arange(images) < live_count[0]).astype(jnp.float32)[:, None, None]
     rel_onehot = (rel_index.reshape(-1)[:, None] == jnp.arange(TABLE)[None, :]).astype(jnp.float32)
@@ -319,75 +356,61 @@
     mask_add = jnp.where(region[:, :, None] == region[:, None, :], 0.0, mask_fill).astype(
         jnp.float32
     )
+    wide = (2, 5, 9, 11)
+    narrow = tuple(member for member in range(13) if member not in wide)
+    widths = [params[member].shape[1] for member in narrow]
+    starts = [sum(widths[:place]) for place in range(len(widths))]
+    small_all = gather_blocks(
+        jnp.concatenate([params[member] for member in narrow], axis=1), devices, 1
+    )
+    weights_all = []
+    for layer_index in range(LAYERS):
+        weights = [None] * 13
+        for turn, member in enumerate(wide):
+            gathered = gather_blocks(params[member][layer_index], devices, turn % 3)
+            weights[member] = gathered.reshape((-1, gathered.shape[-1]))
+        for member, start, width in zip(narrow, starts, widths):
+            weights[member] = small_all[:, layer_index, start : start + width].reshape(-1)
+        weights_all.append(tuple(weights))
     stream = tokens
     saved_all = []
-    gathered_all = []
     for layer_index in range(LAYERS):
-        weights = (
-            lax.all_gather(norm1_gain[layer_index], "fsdp", axis=0, tiled=True),
-            lax.all_gather(norm1_bias[layer_index], "fsdp", axis=0, tiled=True),
-            lax.all_gather(qkv_weight[layer_index], "fsdp", axis=0, tiled=True),
-            lax.all_gather(qv_bias[layer_index], "fsdp", axis=0, tiled=True),
-            lax.all_gather(bias_table[layer_index], "fsdp", axis=0, tiled=True),
-            lax.all_gather(proj_weight[layer_index], "fsdp", axis=0, tiled=True),
-            lax.all_gather(proj_bias[layer_index], "fsdp", axis=0, tiled=True),
-            lax.all_gather(norm2_gain[layer_index], "fsdp", axis=0, tiled=True),
-            lax.all_gather(norm2_bias[layer_index], "fsdp", axis=0, tiled=True),
-            lax.all_gather(fc1_weight[layer_index], "fsdp", axis=0, tiled=True),
-            lax.all_gather(fc1_bias[layer_index], "fsdp", axis=0, tiled=True),
-            lax.all_gather(fc2_weight[layer_index], "fsdp", axis=0, tiled=True),
-            lax.all_gather(fc2_bias[layer_index], "fsdp", axis=0, tiled=True),
-        )
         shifted = layer_index % 2 == 1
         stream, saved_state = layer_forward(
-            stream, weights, shifted, rel_onehot, mask_add if shifted else None
+            stream, weights_all[layer_index], shifted, rel_onehot, mask_add if shifted else None
         )
         saved_all.append(saved_state)
-        gathered_all.append(weights)
     result = stream * live_rows
     grad_stream = cotangent * live_rows
     layer_grads = [None] * LAYERS
+    small_grads = [None] * LAYERS
     for layer_index in range(LAYERS - 1, -1, -1):
         shifted = layer_index % 2 == 1
-        weights = (
-            lax.all_gather(norm1_gain[layer_index], "fsdp", axis=0, tiled=True),
-            lax.all_gather(norm1_bias[layer_index], "fsdp", axis=0, tiled=True),
-            lax.all_gather(qkv_weight[layer_index], "fsdp", axis=0, tiled=True),
-            lax.all_gather(qv_bias[layer_index], "fsdp", axis=0, tiled=True),
-            lax.all_gather(bias_table[layer_index], "fsdp", axis=0, tiled=True),
-            lax.all_gather(proj_weight[layer_index], "fsdp", axis=0, tiled=True),
-            lax.all_gather(proj_bias[layer_index], "fsdp", axis=0, tiled=True),
-            lax.all_gather(norm2_gain[layer_index], "fsdp", axis=0, tiled=True),
-            lax.all_gather(norm2_bias[layer_index], "fsdp", axis=0, tiled=True),
-            lax.all_gather(fc1_weight[layer_index], "fsdp", axis=0, tiled=True),
-            lax.all_gather(fc1_bias[layer_index], "fsdp", axis=0, tiled=True),
-            lax.all_gather(fc2_weight[layer_index], "fsdp", axis=0, tiled=True),
-            lax.all_gather(fc2_bias[layer_index], "fsdp", axis=0, tiled=True),
-        )
         grad_stream, full_grads = layer_backward(
             grad_stream,
             saved_all[layer_index],
-            weights,
+            weights_all[layer_index],
             shifted,
             rel_onehot,
             mask_add if shifted else None,
         )
-        layer_grads[layer_index] = (
-            lax.psum_scatter(full_grads[0], "fsdp", scatter_dimension=0, tiled=True),
-            lax.psum_scatter(full_grads[1], "fsdp", scatter_dimension=0, tiled=True),
-            lax.psum_scatter(full_grads[2], "fsdp", scatter_dimension=0, tiled=True),
-            lax.psum_scatter(full_grads[3], "fsdp", scatter_dimension=0, tiled=True),
-            lax.psum_scatter(full_grads[4], "fsdp", scatter_dimension=0, tiled=True),
-            lax.psum_scatter(full_grads[5], "fsdp", scatter_dimension=0, tiled=True),
-            lax.psum_scatter(full_grads[6], "fsdp", scatter_dimension=0, tiled=True),
-            lax.psum_scatter(full_grads[7], "fsdp", scatter_dimension=0, tiled=True),
-            lax.psum_scatter(full_grads[8], "fsdp", scatter_dimension=0, tiled=True),
-            lax.psum_scatter(full_grads[9], "fsdp", scatter_dimension=0, tiled=True),
-            lax.psum_scatter(full_grads[10], "fsdp", scatter_dimension=0, tiled=True),
-            lax.psum_scatter(full_grads[11], "fsdp", scatter_dimension=0, tiled=True),
-            lax.psum_scatter(full_grads[12], "fsdp", scatter_dimension=0, tiled=True),
+        layer_grads[layer_index] = {}
+        for turn, member in enumerate(wide):
+            full = full_grads[member].astype(jnp.bfloat16)
+            layer_grads[layer_index][member] = scatter_sums(
+                full.reshape(devices, -1, full.shape[-1]), devices, turn % 3, jnp.bfloat16
+            )
+        small_grads[layer_index] = jnp.concatenate(
+            [full_grads[member].reshape(devices, -1) for member in narrow], axis=1
         )
-    finished = tuple((stack_member(layer_grads, member) for member in range(13)))
+    small_sums = scatter_sums(jnp.stack(small_grads, axis=1), devices, 1, jnp.float32)
+    finished = []
+    for member in range(13):
+        if member in wide:
+            finished.append(jnp.stack([grads[member] for grads in layer_grads]))
+        else:
+            place = narrow.index(member)
+            finished.append(small_sums[:, starts[place] : starts[place] + widths[place]])
     return (result, grad_stream) + tuple(finished)
 
 
@@ -429,4 +452,5 @@
         P(None, "fsdp", None),
         P(None, "fsdp"),
     )
-    return jax.shard_map(shards, mesh=mesh, in_specs=in_specs, out_specs=out_specs, check_vma=False)
+    devices = mesh.shape["fsdp"]
+    return jax.shard_map(functools.partial(shards, devices), mesh=mesh, in_specs=in_specs, out_specs=out_specs, check_vma=False)

time: 1880 us -> 923 us (0.49)
  waiting for transfers between devices: 1120 us -> 139 us
  blocking collectives: 129 us -> 0 us
  local copies, waits for them, and re-layouts: 269 us -> 367 us
  starting transfers between devices: 0.78 us -> 85.8 us
  matrix products: 235 us -> 203 us
    reduce_scatter x8 -> x0, waiting for transfers between devices: 1020 us -> none  [the longest x2 280 us: shards(): lax.psum_scatter(full_grads[9], 'fsdp', scatter_dimension=0, tiled=True)]
    ppermute x0 -> x90, waiting for transfers between devices: none -> 139 us  [the longest x45 85.1 us: scatter_sums(): arrived = lax.ppermute(away, 'fsdp', partner_pairs(devices, bit))]
    unnamed x16 -> x0, waiting for transfers between devices: 95.1 us -> none
    all_gather x2 -> x0, blocking collectives: 86.2 us -> none  [shards(): lax.all_gather(proj_weight[layer_index], 'fsdp', axis=0, tiled=True)]
    ppermute x0 -> x90, starting transfers between devices: none -> 85.8 us  [the longest x45 48 us: gather_blocks(): other = lax.ppermute(block, 'fsdp', partner_pairs(devices, bit))]
    concatenate x2 -> x12, local copies, waits for them, and re-layouts: 4.53 us -> 73.9 us  [layer_backward(): jnp.concatenate([grad_queries.reshape(-1, features), grad_keys.reshape(-1...]
    unnamed x1 -> x0, blocking collectives: 42.9 us -> none
  transfers between devices with their start and end apart: 15 -> 90, of which waited for: 9 -> 42; matrix products, arithmetic and copies ran while one was open for 17% -> 39% of each run, Pallas kernels for 0% -> 0%
where the time goes in v1:
time: 923 us; the launch traced here: 913 us
  local copies, waits for them, and re-layouts  367 us (40%)
  matrix products  203 us (22%)
  waiting for transfers between devices  139 us (15%)
  other arithmetic  113 us (12%)
  starting transfers between devices  85.8 us (9%)
    ppermute x45, waiting for transfers between devices, scatter_sums(): arrived = lax.ppermute(away, 'fsdp', partner_pairs(devices, bit))  85.1 us
    concatenate x12, local copies, waits for them, and re-layouts, layer_backward(): jnp.concatenate([grad_queries.reshape(-1, features), grad_keys.reshape(-1...  73.9 us
    ppermute x45, waiting for transfers between devices, gather_blocks(): other = lax.ppermute(block, 'fsdp', partner_pairs(devices, bit))  53.8 us
    ppermute x45, starting transfers between devices, gather_blocks(): other = lax.ppermute(block, 'fsdp', partner_pairs(devices, bit))  48 us
    dot_general x2, matrix products, layer_forward(): jnp.dot(normed_two.reshape(-1, features), up_w, preferred_element_type=jn...  42.9 us
    dot_general x8, matrix products, times_transposed(): lax.dot_general(rows_left, rows_right, (((1,), (1,)), ((), ())), preferre...  39.2 us
    ppermute x45, starting transfers between devices, scatter_sums(): arrived = lax.ppermute(away, 'fsdp', partner_pairs(devices, bit))  37.7 us
    dot_general x10, matrix products, contract_rows(): lax.dot_general(rows_left, rows_right, (((0,), (0,)), ((), ())), precisio...  35 us
  transfers between devices with their start and end apart: 90, of which 42 were waited for; matrix products, arithmetic and copies ran while one was open for 39% of the time, Pallas kernels for 0%

profile of v1, /device:TPU:0, one launch (start us, length us, event | category | flops | bytes accessed | tf_op | source)
XLA Modules:
  0.0 913.0 jit_solution(11924616837221435178)
XLA Ops:
  120.5 8.2 collective-permute-done.28
  129.8 10.1 %collective-permute-done.23 = bf16[2,2,2,64,512]{4,3,2,1,0:T(8,128)(2,1)S(1)} collective-permute-done((bf16[2,2,2,64,512]{4,3,2,1,0:T(8,128)(2,1)S(1)}, bf16[2,2,2,64,512]{4,3,2,1,0:T(8,128)(2,1)S(1)}, u32[]{:S(2)}, u32[]{:S(2)}) %collective-permute-start.23) | collective-permute-done | bytes 524320 | tf_op jit(solution)/shard_map/ppermute | solution.py:314
  141.1 9.6 %collective-permute-done.43 = bf16[2,2,2,64,512]{4,3,2,1,0:T(8,128)(2,1)S(1)} collective-permute-done((bf16[2,2,2,64,512]{4,3,2,1,0:T(8,128)(2,1)S(1)}, bf16[2,2,2,64,512]{4,3,2,1,0:T(8,128)(2,1)S(1)}, u32[]{:S(2)}, u32[]{:S(2)}) %collective-permute-start.43) | collective-permute-done | bytes 524320 | tf_op jit(solution)/shard_map/ppermute | solution.py:314
  179.9 6.6 copy.316
  192.3 6.6 copy.319
  243.6 21.7 %multiply_convert_fusion.1 = (bf16[980,2048]{1,0:T(8,128)(2,1)S(1)}, f32[980,2048]{1,0:T(8,128)}, f32[980,2048]{1,0:T(8,128)}) fusion(f32[2048]{0:T(1024)S(1)} %copy-done.139, bf16[980,512]{1,0:T(8,128)(2,1)S(1)} %copy-done.82, bf16[512,2048]{1,0:T(8,128)(2,1)S(1)} %bitcast.741), kind=kOutput, calls=%fused_computation.29 | convolution fusion | flops 2187673600 | bytes 23179264 | tf_op jit(solution)/shard_map/dot_general | solution.py:149
  294.3 6.7 copy.341
  305.1 6.7 copy.342
  315.9 6.8 copy.346
  372.3 21.3 %multiply_convert_fusion = (bf16[980,2048]{1,0:T(8,128)(2,1)}, f32[980,2048]{1,0:T(8,128)S(1)}, f32[980,2048]{1,0:T(8,128)S(1)}) fusion(f32[2048]{0:T(1024)S(1)} %copy-done.141, bf16[980,512]{1,0:T(8,128)(2,1)S(1)} %reshape.675, bf16[512,2048]{1,0:T(8,128)(2,1)} %bitcast.747), kind=kOutput, calls=%fused_computation.16 | convolution fusion | flops 2187673600 | bytes 23179264 | tf_op jit(solution)/shard_map/dot_general | solution.py:149
  452.1 6.7 copy.363
  458.8 12.4 %multiply_reduce_fusion.1 = (f32[20,16,49]{2,1,0:T(8,128)S(1)}, f32[20,16,49,49]{2,3,1,0:T(8,128)}) fusion(f32[20,16,49,49]{2,3,1,0:T(8,128)} %copy-done.1, f32[20,16,49]{2,1,0:T(8,128)S(1)} %log_add_fusion, f32[20,49,49]{1,2,0:T(8,128)S(1)} %bitcast.723, f32[16,49,49]{1,2,0:T(8,128)S(1)} %copy-done.25, bf16[20,49,16,32]{1,3,2,0:T(8,128)(2,1)} %copy.363, ...), kind=kOutput, calls=%fused_computation.5 | convolution fusion | flops 52998400 | bytes 8624784 | tf_op jit(solution)/shard_map/wqhc,wkhc->whqk/dot_general | solution.py:233
  476.9 6.9 fusion.185
  505.2 6.8 copy.440
  566.2 9.0 fusion.196
  603.0 6.7 copy.380
  609.8 11.4 %multiply_reduce_fusion = (f32[20,16,49]{2,1,0:T(8,128)S(1)}, f32[20,16,49,49]{2,3,1,0:T(8,128)}) fusion(f32[20,16,49,49]{2,3,1,0:T(8,128)} %copy-done, f32[20,16,49]{2,1,0:T(8,128)} %copy-done.52, f32[16,49,49]{1,2,0:T(8,128)} %copy-done.23, bf16[20,49,16,32]{1,3,2,0:T(8,128)(2,1)} %copy.380, bf16[20,49,16,32]{1,3,2,0:T(8,128)(2,1)S(1)} %copy-done.14), kind=kOutput, calls=%fused_computation.3 | convolution fusion | flops 52230080 | bytes 8432704 | tf_op jit(solution)/shard_map/wqhc,wkhc->whqk/dot_general | solution.py:233
  626.2 7.3 fusion.189
  646.3 6.6 copy.442
  658.1 6.6 copy.443
  724.3 6.8 reshape.753
  733.9 6.7 reshape.754
  743.3 6.6 reshape.755
  846.9 8.2 collective-permute-done.51
  (940 shorter events, 695.2 us)
Async XLA Ops:
  10.8 55.1 %collective-permute-start.25 = (bf16[16,1536]{1,0:T(8,128)(2,1)}, bf16[16,1536]{1,0:T(8,128)(2,1)}, u32[]{:S(2)}, u32[]{:S(2)}) collective-permute-start(bf16[16,1536]{1,0:T(8,128)(2,1)} %get-tuple-element.182), channel_id=1, source_target_pairs={{0,16},{1,17},{2,18},{3,19},{4,20},{5,21},{6,22},{7,23},{8,24},{9,... | collective-permute-start | bytes 147464 | tf_op jit(solution)/shard_map/ppermute | solution.py:314
  10.8 57.8 %collective-permute-start.5 = (bf16[16,1536]{1,0:T(8,128)(2,1)}, bf16[16,1536]{1,0:T(8,128)(2,1)}, u32[]{:S(2)}, u32[]{:S(2)}) collective-permute-start(bf16[16,1536]{1,0:T(8,128)(2,1)} %get-tuple-element.183), channel_id=1, source_target_pairs={{0,16},{1,17},{2,18},{3,19},{4,20},{5,21},{6,22},{7,23},{8,24},{9,... | collective-permute-start | bytes 147464 | tf_op jit(solution)/shard_map/ppermute | solution.py:314
  30.8 43.3 %collective-permute-start.35 = (bf16[16,2048]{1,0:T(8,128)(2,1)}, bf16[16,2048]{1,0:T(8,128)(2,1)}, u32[]{:S(2)}, u32[]{:S(2)}) collective-permute-start(bf16[16,2048]{1,0:T(8,128)(2,1)} %get-tuple-element.172), channel_id=1, source_target_pairs={{0,16},{1,17},{2,18},{3,19},{4,20},{5,21},{6,22},{7,23},{8,24},{9,... | collective-permute-start | bytes 196616 | tf_op jit(solution)/shard_map/ppermute | solution.py:314
  33.5 28.6 %collective-permute-start.11 = (bf16[2,16,512]{2,1,0:T(8,128)(2,1)}, bf16[2,16,512]{2,1,0:T(8,128)(2,1)}, u32[]{:S(2)}, u32[]{:S(2)}) collective-permute-start(bf16[2,16,512]{2,1,0:T(8,128)(2,1)} %pad_maximum_fusion.51), channel_id=1, source_target_pairs={{0,8},{1,9},{2,10},{3,11},{4,12},{5,13},{6,14},{7,15},{8,0},{9,1},... | collective-permute-start | bytes 98312 | tf_op jit(solution)/shard_map/ppermute | solution.py:314
  36.4 28.3 %collective-permute-start.31 = (bf16[2,16,512]{2,1,0:T(8,128)(2,1)}, bf16[2,16,512]{2,1,0:T(8,128)(2,1)}, u32[]{:S(2)}, u32[]{:S(2)}) collective-permute-start(bf16[2,16,512]{2,1,0:T(8,128)(2,1)} %pad_maximum_fusion.52), channel_id=1, source_target_pairs={{0,8},{1,9},{2,10},{3,11},{4,12},{5,13},{6,14},{7,15},{8,0},{9,1},... | collective-permute-start | bytes 98312 | tf_op jit(solution)/shard_map/ppermute | solution.py:314
  112.5 27.4 %collective-permute-start.23 = (bf16[2,2,2,64,512]{4,3,2,1,0:T(8,128)(2,1)S(1)}, bf16[2,2,2,64,512]{4,3,2,1,0:T(8,128)(2,1)S(1)}, u32[]{:S(2)}, u32[]{:S(2)}) collective-permute-start(bf16[2,2,2,64,512]{4,3,2,1,0:T(8,128)(2,1)S(1)} %pad_maximum_fusion.22), channel_id=1, source_target_pairs={{0,2},{1,3},{2,0},{3,1},{4,6},{5,7},{6,4},{7,5},{8,10},{9,11},{10,... | collective-permute-start | bytes 1572872 | tf_op jit(solution)/shard_map/ppermute | solution.py:314
  113.6 37.2 %collective-permute-start.43 = (bf16[2,2,2,64,512]{4,3,2,1,0:T(8,128)(2,1)S(1)}, bf16[2,2,2,64,512]{4,3,2,1,0:T(8,128)(2,1)S(1)}, u32[]{:S(2)}, u32[]{:S(2)}) collective-permute-start(bf16[2,2,2,64,512]{4,3,2,1,0:T(8,128)(2,1)S(1)} %pad_maximum_fusion.25), channel_id=1, source_target_pairs={{0,2},{1,3},{2,0},{3,1},{4,6},{5,7},{6,4},{7,5},{8,10},{9,11},{10,... | collective-permute-start | bytes 1572872 | tf_op jit(solution)/shard_map/ppermute | solution.py:314
  115.7 37.0 %collective-permute-start.18 = (bf16[2,2,2,16,2048]{4,3,0,1,2:T(8,128)(2,1)S(1)}, bf16[2,2,2,16,2048]{4,3,0,1,2:T(8,128)(2,1)S(1)}, u32[]{:S(2)}, u32[]{:S(2)}) collective-permute-start(bf16[2,2,2,16,2048]{4,3,0,1,2:T(8,128)(2,1)S(1)} %pad_maximum_fusion.21), channel_id=1, source_target_pairs={{0,8},{1,9},{2,10},{3,11},{4,12},{5,13},{6,14},{7,15},{8,0},{9,1},... | collective-permute-start | bytes 1572872 | tf_op jit(solution)/shard_map/ppermute | solution.py:314
  120.3 33.0 %collective-permute-start.38 = (bf16[2,2,2,16,2048]{4,3,0,1,2:T(8,128)(2,1)S(1)}, bf16[2,2,2,16,2048]{4,3,0,1,2:T(8,128)(2,1)S(1)}, u32[]{:S(2)}, u32[]{:S(2)}) collective-permute-start(bf16[2,2,2,16,2048]{4,3,0,1,2:T(8,128)(2,1)S(1)} %pad_maximum_fusion.24), channel_id=1, source_target_pairs={{0,8},{1,9},{2,10},{3,11},{4,12},{5,13},{6,14},{7,15},{8,0},{9,1},... | collective-permute-start | bytes 1572872 | tf_op jit(solution)/shard_map/ppermute | solution.py:314
  128.7 27.1 %collective-permute-start.9 = (bf16[2,2,2,2,16,1536]{5,4,0,1,2,3:T(8,128)(2,1)S(1)}, bf16[2,2,2,2,16,1536]{5,4,0,1,2,3:T(8,128)(2,1)S(1)}, u32[]{:S(2)}, u32[]{:S(2)}) collective-permute-start(bf16[2,2,2,2,16,1536]{5,4,0,1,2,3:T(8,128)(2,1)S(1)} %pad_maximum_fusion.16), channel_id=1, source_target_pairs={{0,1},{1,0},{2,3},{3,2},{4,5},{5,4},{6,7},{7,6},{8,9},{9,8},{10,11... | collective-permute-start | bytes 2359304 | tf_op jit(solution)/shard_map/ppermute | solution.py:314
  139.9 92.9 %collective-permute-start.29 = (bf16[2,2,2,2,16,1536]{5,4,0,1,2,3:T(8,128)(2,1)}, bf16[2,2,2,2,16,1536]{5,4,0,1,2,3:T(8,128)(2,1)}, u32[]{:S(2)}, u32[]{:S(2)}) collective-permute-start(bf16[2,2,2,2,16,1536]{5,4,0,1,2,3:T(8,128)(2,1)} %pad_maximum_fusion.17), channel_id=1, source_target_pairs={{0,1},{1,0},{2,3},{3,2},{4,5},{5,4},{6,7},{7,6},{8,9},{9,8},{10,11... | collective-permute-start | bytes 2359304 | tf_op jit(solution)/shard_map/ppermute | solution.py:314
  150.8 89.3 %collective-permute-start.24 = (bf16[2,2,2,2,64,512]{5,4,3,2,1,0:T(8,128)(2,1)}, bf16[2,2,2,2,64,512]{5,4,3,2,1,0:T(8,128)(2,1)}, u32[]{:S(2)}, u32[]{:S(2)}) collective-permute-start(bf16[2,2,2,2,64,512]{5,4,3,2,1,0:T(8,128)(2,1)} %pad_maximum_fusion.13), channel_id=1, source_target_pairs={{0,1},{1,0},{2,3},{3,2},{4,5},{5,4},{6,7},{7,6},{8,9},{9,8},{10,11... | collective-permute-start | bytes 3145736 | tf_op jit(solution)/shard_map/ppermute | solution.py:314
  152.8 202.7 %collective-permute-start.44 = (bf16[2,2,2,2,64,512]{5,4,3,2,1,0:T(8,128)(2,1)}, bf16[2,2,2,2,64,512]{5,4,3,2,1,0:T(8,128)(2,1)}, u32[]{:S(2)}, u32[]{:S(2)}) collective-permute-start(bf16[2,2,2,2,64,512]{5,4,3,2,1,0:T(8,128)(2,1)} %pad_maximum_fusion.15), channel_id=1, source_target_pairs={{0,1},{1,0},{2,3},{3,2},{4,5},{5,4},{6,7},{7,6},{8,9},{9,8},{10,11... | collective-permute-start | bytes 3145736 | tf_op jit(solution)/shard_map/ppermute | solution.py:314
  154.6 83.6 %collective-permute-start.19 = (bf16[2,2,2,2,16,2048]{5,4,0,2,3,1:T(8,128)(2,1)}, bf16[2,2,2,2,16,2048]{5,4,0,2,3,1:T(8,128)(2,1)}, u32[]{:S(2)}, u32[]{:S(2)}) collective-permute-start(bf16[2,2,2,2,16,2048]{5,4,0,2,3,1:T(8,128)(2,1)} %pad_maximum_fusion.12), channel_id=1, source_target_pairs={{0,1},{1,0},{2,3},{3,2},{4,5},{5,4},{6,7},{7,6},{8,9},{9,8},{10,11... | collective-permute-start | bytes 3145736 | tf_op jit(solution)/shard_map/ppermute | solution.py:314
  155.7 204.1 %collective-permute-start.39 = (bf16[2,2,2,2,16,2048]{5,4,0,2,3,1:T(8,128)(2,1)}, bf16[2,2,2,2,16,2048]{5,4,0,2,3,1:T(8,128)(2,1)}, u32[]{:S(2)}, u32[]{:S(2)}) collective-permute-start(bf16[2,2,2,2,16,2048]{5,4,0,2,3,1:T(8,128)(2,1)} %pad_maximum_fusion.14), channel_id=1, source_target_pairs={{0,1},{1,0},{2,3},{3,2},{4,5},{5,4},{6,7},{7,6},{8,9},{9,8},{10,11... | collective-permute-start | bytes 3145736 | tf_op jit(solution)/shard_map/ppermute | solution.py:314
  677.2 158.8 %collective-permute-start.85 = (bf16[2,2,2,2,64,512]{5,4,0,1,2,3:T(8,128)(2,1)}, bf16[2,2,2,2,64,512]{5,4,0,1,2,3:T(8,128)(2,1)}, u32[]{:S(2)}, u32[]{:S(2)}) collective-permute-start(bf16[2,2,2,2,64,512]{5,4,0,1,2,3:T(8,128)(2,1)} %bitcast.705), channel_id=1, source_target_pairs={{0,1},{1,0},{2,3},{3,2},{4,5},{5,4},{6,7},{7,6},{8,9},{9,8},{10,11... | collective-permute-start | bytes 3145736 | tf_op jit(solution)/shard_map/ppermute | solution.py:335
  679.7 159.0 %collective-permute-start.75 = (bf16[2,2,2,2,16,2048]{5,4,0,2,3,1:T(8,128)(2,1)}, bf16[2,2,2,2,16,2048]{5,4,0,2,3,1:T(8,128)(2,1)}, u32[]{:S(2)}, u32[]{:S(2)}) collective-permute-start(bf16[2,2,2,2,16,2048]{5,4,0,2,3,1:T(8,128)(2,1)} %bitcast.707), channel_id=1, source_target_pairs={{0,1},{1,0},{2,3},{3,2},{4,5},{5,4},{6,7},{7,6},{8,9},{9,8},{10,11... | collective-permute-start | bytes 3145736 | tf_op jit(solution)/shard_map/ppermute | solution.py:335
  681.0 112.5 %collective-permute-start.65 = (bf16[2,2,2,2,16,512]{5,4,0,1,3,2:T(8,128)(2,1)}, bf16[2,2,2,2,16,512]{5,4,0,1,3,2:T(8,128)(2,1)}, u32[]{:S(2)}, u32[]{:S(2)}) collective-permute-start(bf16[2,2,2,2,16,512]{5,4,0,1,3,2:T(8,128)(2,1)} %bitcast.711), channel_id=1, source_target_pairs={{0,1},{1,0},{2,3},{3,2},{4,5},{5,4},{6,7},{7,6},{8,9},{9,8},{10,11... | collective-permute-start | bytes 786440 | tf_op jit(solution)/shard_map/ppermute | solution.py:335
  708.0 124.5 %collective-permute-start.55 = (bf16[2,2,2,2,16,1536]{5,4,0,1,2,3:T(8,128)(2,1)}, bf16[2,2,2,2,16,1536]{5,4,0,1,2,3:T(8,128)(2,1)}, u32[]{:S(2)}, u32[]{:S(2)}) collective-permute-start(bf16[2,2,2,2,16,1536]{5,4,0,1,2,3:T(8,128)(2,1)} %bitcast.709), channel_id=1, source_target_pairs={{0,1},{1,0},{2,3},{3,2},{4,5},{5,4},{6,7},{7,6},{8,9},{9,8},{10,11... | collective-permute-start | bytes 2359304 | tf_op jit(solution)/shard_map/ppermute | solution.py:335
  791.0 50.5 %collective-permute-start.80 = (bf16[2,2,2,2,64,512]{5,4,0,1,2,3:T(8,128)(2,1)S(1)}, bf16[2,2,2,2,64,512]{5,4,0,1,2,3:T(8,128)(2,1)S(1)}, u32[]{:S(2)}, u32[]{:S(2)}) collective-permute-start(bf16[2,2,2,2,64,512]{5,4,0,1,2,3:T(8,128)(2,1)S(1)} %bitcast.758), channel_id=1, source_target_pairs={{0,1},{1,0},{2,3},{3,2},{4,5},{5,4},{6,7},{7,6},{8,9},{9,8},{10,11... | collective-permute-start | bytes 3145736 | tf_op jit(solution)/shard_map/ppermute | solution.py:335
  838.7 49.1 %collective-permute-start.86 = (bf16[2,2,2,64,512]{4,3,0,1,2:T(8,128)(2,1)S(1)}, bf16[2,2,2,64,512]{4,3,0,1,2:T(8,128)(2,1)S(1)}, u32[]{:S(2)}, u32[]{:S(2)}) collective-permute-start(bf16[2,2,2,64,512]{4,3,0,1,2:T(8,128)(2,1)S(1)} %dynamic-slice_bitcast_fusion), channel_id=1, source_target_pairs={{0,2},{1,3},{2,0},{3,1},{4,6},{5,7},{6,4},{7,5},{8,10},{9,11},{10,... | collective-permute-start | bytes 1572872 | tf_op jit(solution)/shard_map/ppermute | solution.py:335
  841.5 48.0 %collective-permute-start.76 = (bf16[2,2,2,16,2048]{4,3,0,1,2:T(8,128)(2,1)S(1)}, bf16[2,2,2,16,2048]{4,3,0,1,2:T(8,128)(2,1)S(1)}, u32[]{:S(2)}, u32[]{:S(2)}) collective-permute-start(bf16[2,2,2,16,2048]{4,3,0,1,2:T(8,128)(2,1)S(1)} %dynamic-slice_bitcast_fusion.2), channel_id=1, source_target_pairs={{0,8},{1,9},{2,10},{3,11},{4,12},{5,13},{6,14},{7,15},{8,0},{9,1},... | collective-permute-start | bytes 1572872 | tf_op jit(solution)/shard_map/ppermute | solution.py:335
  842.1 48.3 %collective-permute-start.81 = (bf16[2,2,2,64,512]{4,3,0,1,2:T(8,128)(2,1)S(1)}, bf16[2,2,2,64,512]{4,3,0,1,2:T(8,128)(2,1)S(1)}, u32[]{:S(2)}, u32[]{:S(2)}) collective-permute-start(bf16[2,2,2,64,512]{4,3,0,1,2:T(8,128)(2,1)S(1)} %dynamic-slice_bitcast_fusion.1), channel_id=1, source_target_pairs={{0,2},{1,3},{2,0},{3,1},{4,6},{5,7},{6,4},{7,5},{8,10},{9,11},{10,... | collective-permute-start | bytes 1572872 | tf_op jit(solution)/shard_map/ppermute | solution.py:335
  846.6 44.6 %collective-permute-start.71 = (bf16[2,2,2,16,2048]{4,3,0,1,2:T(8,128)(2,1)S(1)}, bf16[2,2,2,16,2048]{4,3,0,1,2:T(8,128)(2,1)S(1)}, u32[]{:S(2)}, u32[]{:S(2)}) collective-permute-start(bf16[2,2,2,16,2048]{4,3,0,1,2:T(8,128)(2,1)S(1)} %dynamic-slice_bitcast_fusion.3), channel_id=1, source_target_pairs={{0,8},{1,9},{2,10},{3,11},{4,12},{5,13},{6,14},{7,15},{8,0},{9,1},... | collective-permute-start | bytes 1572872 | tf_op jit(solution)/shard_map/ppermute | solution.py:335
  (230 other events, 1722.0 us)

commit v2 on v1

--- a/solution.py
+++ b/solution.py
@@ -3,6 +3,8 @@
 import jax
 import jax.numpy as jnp
 from jax import lax
+from jax.experimental import pallas as pl
+from jax.experimental.pallas import tpu as pltpu
 from jax.sharding import PartitionSpec as P
 
 HEAD = 32
@@ -16,6 +18,10 @@
 
 norm_eps = 1e-05
 mask_fill = -100.0
+ROWS = 64
+GROUP = 128
+PACK = GROUP // HEAD
+empty_fill = -1e30
 
 
 def to_windows(grid_rows):
@@ -83,17 +89,154 @@
     return lookup.reshape(WIN * WIN, WIN * WIN, HEADS).transpose(2, 0, 1)
 
 
-def attend_scores(queries, keys_low, bias_heads, mask_add):
-    scores = jnp.einsum("wqhc,wkhc->whqk", queries, keys_low, preferred_element_type=jnp.float32)
-    scores = scores + bias_heads[None]
+def window_rows(token_rows, shifted):
+    windows = enter_windows(token_rows, shifted)
+    windows = jnp.pad(windows, ((0, 0), (0, ROWS - WIN * WIN), (0, 0)))
+    return windows.reshape(-1, windows.shape[-1])
+
+
+def token_rows_of(rows, images, shifted):
+    windows = rows.reshape(-1, ROWS, rows.shape[-1])[:, : WIN * WIN]
+    return leave_windows(windows, images, shifted)
+
+
+def padded_bias(table_flat, rel_onehot):
+    bias = position_bias(table_flat, rel_onehot)
+    spare = ROWS - WIN * WIN
+    bias = jnp.pad(bias, ((0, 0), (0, spare), (0, 0)))
+    bias = jnp.pad(bias, ((0, 0), (0, 0), (0, spare)), constant_values=empty_fill)
+    return bias.reshape(HEADS * ROWS, ROWS)
+
+
+def head_masks():
+    lane = lax.broadcasted_iota(jnp.int32, (ROWS, GROUP), 1) // HEAD
+    return [(lane == head).astype(jnp.float32) for head in range(PACK)]
+
+
+def stack_heads(rows, masks):
+    wide = rows.astype(jnp.float32)
+    return jnp.concatenate([wide * mask for mask in masks], axis=0).astype(jnp.bfloat16)
+
+
+def merge_heads(stacked, masks):
+    total = stacked[:ROWS] * masks[0]
+    for head in range(1, PACK):
+        total = total + stacked[head * ROWS : (head + 1) * ROWS] * masks[head]
+    return total
+
+
+def dot_rows(left, right):
+    return lax.dot_general(
+        left, right, (((1,), (1,)), ((), ())), preferred_element_type=jnp.float32
+    )
+
+
+def group_probs(stacked, keys, bias_ref, mask_ref, group):
+    scores = dot_rows(stacked, keys)
+    scores = scores + bias_ref[group * PACK * ROWS : (group + 1) * PACK * ROWS, :]
+    if mask_ref is not None:
+        scores = scores + jnp.concatenate([mask_ref[0]] * PACK, axis=0)
+    top = jnp.max(scores, axis=-1, keepdims=True)
+    powers = jnp.exp(scores - top)
+    return powers / jnp.sum(powers, axis=-1, keepdims=True)
+
+
+def attend_kernel(features, has_mask, qkv_ref, bias_ref, *refs):
+    mask_ref = refs[0] if has_mask else None
+    out_ref = refs[-1]
+    masks = head_masks()
+    for group in range(features // GROUP):
+        low = group * GROUP
+        stacked = stack_heads(qkv_ref[:, low : low + GROUP], masks)
+        keys = qkv_ref[:, features + low : features + low + GROUP]
+        values = qkv_ref[:, 2 * features + low : 2 * features + low + GROUP]
+        probs = group_probs(stacked, keys, bias_ref, mask_ref, group).astype(jnp.bfloat16)
+        spread = jnp.dot(probs, values, preferred_element_type=jnp.float32)
+        out_ref[:, low : low + GROUP] = merge_heads(spread, masks).astype(jnp.bfloat16)
+
+
+def attend_back_kernel(features, has_mask, qkv_ref, grad_ref, bias_ref, *refs):
+    mask_ref = refs[0] if has_mask else None
+    out_ref, sums_ref, bias_grad_ref = refs[-3:]
+    masks = head_masks()
+
+    @pl.when(pl.program_id(0) == 0)
+    def _():
+        sums_ref[...] = jnp.zeros_like(sums_ref)
+        bias_grad_ref[...] = jnp.zeros_like(bias_grad_ref)
+
+    def put(part, low, value):
+        at = part * features + low
+        out_ref[:, at : at + GROUP] = value.astype(jnp.bfloat16)
+        sums_ref[:, at : at + GROUP] += jnp.sum(value, axis=0, keepdims=True)
+
+    for group in range(features // GROUP):
+        low = group * GROUP
+        rows = slice(group * PACK * ROWS, (group + 1) * PACK * ROWS)
+        stacked = stack_heads(qkv_ref[:, low : low + GROUP], masks)
+        grads = stack_heads(grad_ref[:, low : low + GROUP], masks)
+        keys = qkv_ref[:, features + low : features + low + GROUP]
+        values = qkv_ref[:, 2 * features + low : 2 * features + low + GROUP]
+        probs = group_probs(stacked, keys, bias_ref, mask_ref, group)
+        grad_probs = dot_rows(grads, values)
+        grad_scores = probs * (
+            grad_probs - jnp.sum(grad_probs * probs, axis=-1, keepdims=True)
+        )
+        bias_grad_ref[rows, :] += grad_scores
+        low_scores = grad_scores.astype(jnp.bfloat16)
+        put(2, low, contract_rows(probs.astype(jnp.bfloat16), grads))
+        put(1, low, contract_rows(low_scores, stacked))
+        spread = jnp.dot(low_scores, keys, preferred_element_type=jnp.float32)
+        put(0, low, merge_heads(spread, masks) * HEAD ** (-0.5))
+
+
+def attention_specs(features, bias_rows, mask_add):
+    specs = [pl.BlockSpec((ROWS, 3 * features), lambda step: (step, 0))]
+    last = [pl.BlockSpec(bias_rows.shape, lambda step: (0, 0))]
+    operands = [bias_rows]
     if mask_add is not None:
-        window_count = scores.shape[0]
-        per_image = mask_add.shape[0]
-        scores = (
-            scores.reshape(window_count // per_image, per_image, HEADS, WIN * WIN, WIN * WIN)
-            + mask_add[None, :, None]
-        ).reshape(scores.shape)
-    return scores
+        count = mask_add.shape[0]
+        last.append(pl.BlockSpec((1, ROWS, ROWS), lambda step: (step % count, 0, 0)))
+        operands.append(mask_add)
+    return specs, last, operands
+
+
+def attend_windows(qkv_low, bias_rows, mask_add):
+    features = qkv_low.shape[1] // 3
+    steps = qkv_low.shape[0] // ROWS
+    first, last, operands = attention_specs(features, bias_rows, mask_add)
+    return pl.pallas_call(
+        functools.partial(attend_kernel, features, mask_add is not None),
+        grid=(steps,),
+        in_specs=first + last,
+        out_specs=pl.BlockSpec((ROWS, features), lambda step: (step, 0)),
+        out_shape=jax.ShapeDtypeStruct((steps * ROWS, features), jnp.bfloat16),
+        compiler_params=pltpu.CompilerParams(vmem_limit_bytes=24 * 1024 * 1024),
+        cost_estimate=pl.CostEstimate(flops=4 * steps * ROWS * ROWS * features * 4, bytes_accessed=8 * steps * ROWS * features, transcendentals=steps * HEADS * ROWS * ROWS),
+    )(qkv_low, *operands)
+
+
+def attend_windows_back(qkv_low, grad_low, bias_rows, mask_add):
+    features = qkv_low.shape[1] // 3
+    steps = qkv_low.shape[0] // ROWS
+    first, last, operands = attention_specs(features, bias_rows, mask_add)
+    return pl.pallas_call(
+        functools.partial(attend_back_kernel, features, mask_add is not None),
+        grid=(steps,),
+        in_specs=first + [pl.BlockSpec((ROWS, features), lambda step: (step, 0))] + last,
+        out_specs=(
+            pl.BlockSpec((ROWS, 3 * features), lambda step: (step, 0)),
+            pl.BlockSpec((1, 3 * features), lambda step: (0, 0)),
+            pl.BlockSpec(bias_rows.shape, lambda step: (0, 0)),
+        ),
+        out_shape=(
+            jax.ShapeDtypeStruct((steps * ROWS, 3 * features), jnp.bfloat16),
+            jax.ShapeDtypeStruct((1, 3 * features), jnp.float32),
+            jax.ShapeDtypeStruct(bias_rows.shape, jnp.float32),
+        ),
+        compiler_params=pltpu.CompilerParams(vmem_limit_bytes=24 * 1024 * 1024),
+        cost_estimate=pl.CostEstimate(flops=10 * steps * ROWS * ROWS * features * 4, bytes_accessed=14 * steps * ROWS * features, transcendentals=steps * HEADS * ROWS * ROWS),
+    )(qkv_low, grad_low, *operands)
 
 
 def layer_forward(stream, weights, shifted, rel_onehot, mask_add):
@@ -117,32 +260,21 @@
     normed_one = layer_norm(
         stream, gain_one.astype(jnp.float32), offset_one.astype(jnp.float32)
     ).astype(jnp.bfloat16)
-    windows = enter_windows(normed_one, shifted).reshape(-1, features)
-    window_count = windows.shape[0] // (WIN * WIN)
+    windows = window_rows(normed_one, shifted)
     qv_float = qv_b.astype(jnp.float32)
+    head_scale = HEAD ** (-0.5)
     qkv = jnp.dot(windows, qkv_w, preferred_element_type=jnp.float32)
     qkv = qkv + jnp.concatenate(
         [qv_float[:features], jnp.zeros((features,), jnp.float32), qv_float[features:]]
     )
-    head_shape = (window_count, WIN * WIN, HEADS, HEAD)
-    head_scale = HEAD ** (-0.5)
-    queries = (qkv[:, :features] * head_scale).astype(jnp.bfloat16).reshape(head_shape)
-    keys_low = qkv[:, features : 2 * features].astype(jnp.bfloat16).reshape(head_shape)
-    values_low = qkv[:, 2 * features :].astype(jnp.bfloat16).reshape(head_shape)
-    scores = attend_scores(queries, keys_low, position_bias(table_flat, rel_onehot), mask_add)
-    row_top = jnp.max(scores, axis=-1, keepdims=True)
-    log_total = row_top + jnp.log(jnp.sum(jnp.exp(scores - row_top), axis=-1, keepdims=True))
-    probs_low = jnp.exp(scores - log_total).astype(jnp.bfloat16)
-    attended = jnp.einsum(
-        "whqk,wkhc->wqhc", probs_low, values_low, preferred_element_type=jnp.float32
-    )
-    attended = attended.astype(jnp.bfloat16).reshape(-1, features)
+    qkv_scale = jnp.where(jnp.arange(3 * features) < features, head_scale, 1.0)
+    qkv_low = (qkv * qkv_scale).astype(jnp.bfloat16)
+    bias_rows = padded_bias(table_flat, rel_onehot)
+    attended = attend_windows(qkv_low, bias_rows, mask_add)
     projected = jnp.dot(attended, proj_w, preferred_element_type=jnp.float32) + proj_b.astype(
         jnp.float32
     )
-    stream_mid = stream + leave_windows(
-        projected.reshape(window_count, WIN * WIN, features), images, shifted
-    )
+    stream_mid = stream + token_rows_of(projected, images, shifted)
     normed_two = layer_norm(
         stream_mid, gain_two.astype(jnp.float32), offset_two.astype(jnp.float32)
     ).astype(jnp.bfloat16)
@@ -157,10 +289,8 @@
     saved_state = (
         stream,
         windows,
-        queries,
-        keys_low,
-        values_low,
-        log_total,
+        qkv_low,
+        bias_rows,
         attended,
         stream_mid,
         normed_two,
@@ -189,10 +319,8 @@
     (
         stream,
         windows,
-        queries,
-        keys_low,
-        values_low,
-        log_total,
+        qkv_low,
+        bias_rows,
         attended,
         stream_mid,
         normed_two,
@@ -201,7 +329,6 @@
     ) = saved_state
     images = stream.shape[0]
     features = stream.shape[-1]
-    window_count = windows.shape[0] // (WIN * WIN)
     grad_rows = grad_out.reshape(-1, features)
     grad_down_b = jnp.sum(grad_rows, axis=0)
     grad_low = grad_rows.astype(jnp.bfloat16)
@@ -218,53 +345,20 @@
     )[1]
     part_mid, grad_gain_two, grad_offset_two = norm_pull(grad_normed_two)
     grad_mid = grad_out + part_mid
-    grad_proj = enter_windows(grad_mid, shifted).reshape(-1, features)
+    grad_proj = window_rows(grad_mid, shifted)
     grad_proj_b = jnp.sum(grad_proj, axis=0)
     grad_proj_low = grad_proj.astype(jnp.bfloat16)
     grad_proj_w = contract_rows(attended, grad_proj_low)
-    head_shape = (window_count, WIN * WIN, HEADS, HEAD)
-    grad_attended = times_transposed(grad_proj_low, proj_w).astype(jnp.bfloat16).reshape(head_shape)
-    scores = attend_scores(queries, keys_low, position_bias(table_flat, rel_onehot), mask_add)
-    attn_probs = jnp.exp(scores - log_total)
-    probs_low = attn_probs.astype(jnp.bfloat16)
-    grad_values = jnp.einsum(
-        "whqk,wqhc->wkhc", probs_low, grad_attended, preferred_element_type=jnp.float32
-    )
-    grad_probs = jnp.einsum(
-        "wqhc,wkhc->whqk", grad_attended, values_low, preferred_element_type=jnp.float32
-    )
-    grad_scores = attn_probs * (
-        grad_probs - jnp.sum(grad_probs * attn_probs, axis=-1, keepdims=True)
-    )
-    bias_sum = jnp.sum(grad_scores, axis=0).transpose(1, 2, 0).reshape(WIN * WIN * WIN * WIN, HEADS)
+    grad_attended = times_transposed(grad_proj_low, proj_w).astype(jnp.bfloat16)
+    grad_qkv_low, qkv_sums, bias_sum = attend_windows_back(
+        qkv_low, grad_attended, bias_rows, mask_add
+    )
+    bias_sum = bias_sum.reshape(HEADS, ROWS, ROWS)[:, : WIN * WIN, : WIN * WIN]
+    bias_sum = bias_sum.transpose(1, 2, 0).reshape(WIN * WIN * WIN * WIN, HEADS)
     grad_table = contract_rows(rel_onehot, bias_sum, lax.Precision.HIGHEST).reshape(-1)
-    grad_scores_low = grad_scores.astype(jnp.bfloat16)
-    head_scale = HEAD ** (-0.5)
-    grad_queries = (
-        jnp.einsum("whqk,wkhc->wqhc", grad_scores_low, keys_low, preferred_element_type=jnp.float32)
-        * head_scale
-    )
-    grad_keys = jnp.einsum(
-        "whqk,wqhc->wkhc", grad_scores_low, queries, preferred_element_type=jnp.float32
-    )
-    grad_qkv = jnp.concatenate(
-        [
-            grad_queries.reshape(-1, features),
-            grad_keys.reshape(-1, features),
-            grad_values.reshape(-1, features),
-        ],
-        axis=1,
-    )
-    grad_qv_b = jnp.concatenate(
-        [jnp.sum(grad_qkv[:, :features], axis=0), jnp.sum(grad_qkv[:, 2 * features :], axis=0)]
-    )
-    grad_qkv_low = grad_qkv.astype(jnp.bfloat16)
+    grad_qv_b = jnp.concatenate([qkv_sums[0, :features], qkv_sums[0, 2 * features :]])
     grad_qkv_w = contract_rows(windows, grad_qkv_low)
-    grad_normed_one = leave_windows(
-        times_transposed(grad_qkv_low, qkv_w).reshape(window_count, WIN * WIN, features),
-        images,
-        shifted,
-    )
+    grad_normed_one = token_rows_of(times_transposed(grad_qkv_low, qkv_w), images, shifted)
     norm_pull = jax.vjp(
         layer_norm, stream, gain_one.astype(jnp.float32), offset_one.astype(jnp.float32)
     )[1]
@@ -356,6 +450,8 @@
     mask_add = jnp.where(region[:, :, None] == region[:, None, :], 0.0, mask_fill).astype(
         jnp.float32
     )
+    spare = ROWS - WIN * WIN
+    mask_add = jnp.pad(mask_add, ((0, 0), (0, spare), (0, spare)))
     wide = (2, 5, 9, 11)
     narrow = tuple(member for member in range(13) if member not in wide)
     widths = [params[member].shape[1] for member in narrow]
@@ -363,15 +459,22 @@
     small_all = gather_blocks(
         jnp.concatenate([params[member] for member in narrow], axis=1), devices, 1
     )
-    weights_all = []
+    weights_all = [[None] * 13 for _ in range(LAYERS)]
     for layer_index in range(LAYERS):
-        weights = [None] * 13
-        for turn, member in enumerate(wide):
-            gathered = gather_blocks(params[member][layer_index], devices, turn % 3)
-            weights[member] = gathered.reshape((-1, gathered.shape[-1]))
         for member, start, width in zip(narrow, starts, widths):
-            weights[member] = small_all[:, layer_index, start : start + width].reshape(-1)
-        weights_all.append(tuple(weights))
+            weights_all[layer_index][member] = small_all[
+                :, layer_index, start : start + width
+            ].reshape(-1)
+    before = small_all
+    rounds = [(layer_index, group) for layer_index in range(LAYERS) for group in ((2, 5), (9, 11))]
+    for layer_index, group in rounds:
+        blocks = [params[member][layer_index] for member in group]
+        if layer_index or group[0] != 2:
+            before, *blocks = lax.optimization_barrier((before, *blocks))
+        for turn, (member, block) in enumerate(zip(group, blocks)):
+            gathered = gather_blocks(block, devices, (0, 2)[turn])
+            weights_all[layer_index][member] = gathered.reshape((-1, gathered.shape[-1]))
+        before = weights_all[layer_index][group[0]]
     stream = tokens
     saved_all = []
     for layer_index in range(LAYERS):

time: 923 us -> 747 us (0.81)
  local copies, waits for them, and re-layouts: 367 us -> 167 us
  Pallas kernels: 0 us -> 117 us
  matrix products: 203 us -> 126 us
  other arithmetic: 113 us -> 77.6 us
  waiting for transfers between devices: 139 us -> 173 us
  starting transfers between devices: 85.8 us -> 69.8 us
    pallas_call x0 -> x4, Pallas kernels: none -> 117 us  [the longest x2 81.8 us: attend_windows_back(): pl.pallas_call(functools.partial(attend_back_kernel, features, mask_add i...]
    reshape x26 -> x14, local copies, waits for them, and re-layouts: 119 us -> 36.1 us  [the longest x8 24.3 us: from_windows(): windows.reshape(images, GRID // WIN, GRID // WIN, WIN, WIN, features)]
    concatenate x12 -> x4, local copies, waits for them, and re-layouts: 73.9 us -> 0.31 us  [layer_backward(): jnp.concatenate([qkv_sums[0, :features], qkv_sums[0, 2 * features:]])]
    dot_general x12 -> x0, matrix products: 65.2 us -> none  [the longest x2 23.7 us: layer_backward(): jnp.einsum('wqhc,wkhc->whqk', grad_attended, values_low, preferred_elemen...]
    reduce_sum x8 -> x0, other arithmetic: 35.4 us -> none  [the longest x2 14.2 us: layer_backward(): jnp.sum(grad_scores, axis=0).transpose(1, 2, 0)]
    another operation x11 -> x1, local copies, waits for them, and re-layouts: 34.3 us -> 0.01 us
    ppermute x45, waiting for transfers between devices: 53.8 us -> 79.2 us  [gather_blocks(): other = lax.ppermute(block, 'fsdp', partner_pairs(devices, bit))]
    unnamed x325 -> x293, local copies, waits for them, and re-layouts: 20.4 us -> 30.5 us
  transfers between devices with their start and end apart: 90 -> 90, of which waited for: 42 -> 52; matrix products, arithmetic and copies ran while one was open for 39% -> 19% of each run, Pallas kernels for 0% -> 2%
where the time goes in v2:
time: 747 us; the launch traced here: 735 us
  waiting for transfers between devices  173 us (23%)
  local copies, waits for them, and re-layouts  167 us (22%)
  matrix products  126 us (17%)
  Pallas kernels  117 us (16%)
  other arithmetic  77.6 us (10%)
  starting transfers between devices  69.8 us (9%)
    ppermute x45, waiting for transfers between devices, scatter_sums(): arrived = lax.ppermute(away, 'fsdp', partner_pairs(devices, bit))  94 us
    pallas_call x2, Pallas kernels, attend_windows_back(): pl.pallas_call(functools.partial(attend_back_kernel, features, mask_add i...  81.8 us
    ppermute x45, waiting for transfers between devices, gather_blocks(): other = lax.ppermute(block, 'fsdp', partner_pairs(devices, bit))  79.2 us
    dot_general x2, matrix products, layer_forward(): jnp.dot(normed_two.reshape(-1, features), up_w, preferred_element_type=jn...  42.5 us
    dot_general x8, matrix products, times_transposed(): lax.dot_general(rows_left, rows_right, (((1,), (1,)), ((), ())), preferre...  39.7 us
    ppermute x45, starting transfers between devices, gather_blocks(): other = lax.ppermute(block, 'fsdp', partner_pairs(devices, bit))  39.6 us
    pallas_call x2, Pallas kernels, attend_windows(): pl.pallas_call(functools.partial(attend_kernel, features, mask_add is not...  35.3 us
    unnamed x293, local copies, waits for them, and re-layouts  30.5 us
  transfers between devices with their start and end apart: 90, of which 52 were waited for; matrix products, arithmetic and copies ran while one was open for 19% of the time, Pallas kernels for 2%

profile of v2, /device:TPU:0, one launch (start us, length us, event | category | flops | bytes accessed | tf_op | source)
XLA Modules:
  0.0 735.0 jit_solution(4538061042110458274)
XLA Ops:
  41.3 5.6 collective-permute-done.7
  88.1 5.2 collective-permute-done.15
  111.3 7.3 collective-permute-done.18
  122.3 17.8 %shard_map.289 = bf16[1280,512]{1,0:T(8,128)(2,1)S(1)} custom-call(bf16[1280,1536]{1,0:T(8,128)(2,1)S(1)} %fusion.14.qkv_ref, f32[1024,64]{1,0:T(8,128)S(1)} %bitcast.644), custom_call_target="tpu_custom_call" | custom-call | flops 671088640 | bytes 5242880 | tf_op jit(solution)/shard_map/pallas_call | solution.py:208
  182.7 22.6 %multiply_convert_fusion.1 = (bf16[980,2048]{1,0:T(8,128)(2,1)S(1)}, f32[980,2048]{1,0:T(8,128)}, f32[980,2048]{1,0:T(8,128)}) fusion(f32[2048]{0:T(1024)S(1)} %copy-done.126, bf16[980,512]{1,0:T(8,128)(2,1)S(1)} %reshape.599, bf16[512,2048]{1,0:T(8,128)(2,1)} %bitcast.666), kind=kOutput, calls=%fused_computation.23 | convolution fusion | flops 2187673600 | bytes 23179264 | tf_op jit(solution)/shard_map/dot_general | solution.py:281
  240.0 17.4 %shard_map.290 = bf16[1280,512]{1,0:T(8,128)(2,1)S(1)} custom-call(bf16[1280,1536]{1,0:T(8,128)(2,1)S(1)} %fusion.15.qkv_ref, f32[1024,64]{1,0:T(8,128)S(1)} %bitcast.642, f32[4,64,64]{2,1,0:T(8,128)S(1)} %pad.38.refs_0_), custom_call_target="tpu_custom_call" | custom-call | flops 671088640 | bytes 5242880 | tf_op jit(solution)/shard_map/pallas_call | solution.py:208
  300.8 11.1 %collective-permute-done.38 = bf16[2,2,2,16,2048]{4,3,0,1,2:T(8,128)(2,1)S(1)} collective-permute-done((bf16[2,2,2,16,2048]{4,3,0,1,2:T(8,128)(2,1)S(1)}, bf16[2,2,2,16,2048]{4,3,0,1,2:T(8,128)(2,1)S(1)}, u32[]{:S(2)}, u32[]{:S(2)}) %collective-permute-start.38) | collective-permute-done | bytes 524320 | tf_op jit(solution)/shard_map/ppermute | solution.py:408
  324.3 19.9 %multiply_convert_fusion = (bf16[980,2048]{1,0:T(8,128)(2,1)}, f32[980,2048]{1,0:T(8,128)S(1)}, f32[980,2048]{1,0:T(8,128)S(1)}) fusion(f32[2048]{0:T(1024)S(1)} %copy-done.128, bf16[980,512]{1,0:T(8,128)(2,1)S(1)} %copy-done.65, bf16[512,2048]{1,0:T(8,128)(2,1)S(1)} %bitcast.670), kind=kOutput, calls=%fused_computation.10 | convolution fusion | flops 2187673600 | bytes 23179264 | tf_op jit(solution)/shard_map/dot_general | solution.py:281
  344.2 6.3 fusion.140
  350.6 5.1 dot_general.103
  355.7 5.6 fusion.131
  370.1 4.6 multiply_reduce_fusion.12
  388.5 41.0 %shard_map.291 = (bf16[1280,1536]{1,0:T(8,128)(2,1)S(1)}, f32[1,1536]{1,0:T(1,128)S(1)}, f32[1024,64]{1,0:T(8,128)S(1)}) custom-call(bf16[1280,1536]{1,0:T(8,128)(2,1)S(1)} %copy-done.3, bf16[1280,512]{1,0:T(8,128)(2,1)S(1)} %convolution_convert_fusion.7.grad_ref, f32[1024,64]{1,0:T(8,128)S(1)} %bitcast.643, f32[4,64,64]{2,1,0:T(8,128)S(1)} %pad.38.refs_0_), custom_call_target="tpu_custom_call" | custom-call | flops 1677721600 | bytes 9175040 | tf_op jit(solution)/shard_map/pallas_call | solution.py:223
  462.4 11.4 %fusion.141 = (f32[2048]{0:T(1024)S(1)}, bf16[980,2048]{1,0:T(8,128)(2,1)}) fusion(f32[980,2048]{1,0:T(8,128)} %get-tuple-element.86, bf16[980,512]{1,0:T(8,128)(2,1)} %convert_element_type.763, bf16[2048,512]{1,0:T(8,128)(2,1)} %bitcast.668, f32[980,2048]{1,0:T(8,128)} %get-tuple-element.226, f32[2048]{0:T(1024)S(1)} %copy-done.127), kind=kOutput, calls=%fused_computation.541 | convolution fusion | flops 2087319552 | bytes 23187456 | tf_op jit(solution)/shard_map/dot_general | solution.py:79
  473.8 4.6 dot_general.109
  478.4 6.1 fusion.132
  525.2 40.8 %shard_map.292 = (bf16[1280,1536]{1,0:T(8,128)(2,1)S(1)}, f32[1,1536]{1,0:T(1,128)S(1)}, f32[1024,64]{1,0:T(8,128)S(1)}) custom-call(bf16[1280,1536]{1,0:T(8,128)(2,1)S(1)} %copy-done.1, bf16[1280,512]{1,0:T(8,128)(2,1)S(1)} %convolution_convert_fusion.6.grad_ref, f32[1024,64]{1,0:T(8,128)S(1)} %bitcast.645), custom_call_target="tpu_custom_call" | custom-call | flops 1677721600 | bytes 9175040 | tf_op jit(solution)/shard_map/pallas_call | solution.py:223
  620.4 4.9 collective-permute-done.66
  625.8 4.5 collective-permute-done.61
  664.9 5.1 collective-permute-done.56
  670.7 7.7 %collective-permute-done.51 = bf16[2,2,2,16,1536]{4,3,0,1,2:T(8,128)(2,1)S(1)} collective-permute-done((bf16[2,2,2,16,1536]{4,3,0,1,2:T(8,128)(2,1)S(1)}, bf16[2,2,2,16,1536]{4,3,0,1,2:T(8,128)(2,1)S(1)}, u32[]{:S(2)}, u32[]{:S(2)}) %collective-permute-start.51) | collective-permute-done | bytes 393248 | tf_op jit(solution)/shard_map/ppermute | solution.py:429
  678.9 5.2 collective-permute-done.57
  684.6 5.2 collective-permute-done.52
  689.9 4.9 collective-permute-done.58
  (859 shorter events, 460.4 us)
Async XLA Ops:
  1.6 16.7 %collective-permute-start = (bf16[2,280]{1,0:T(2,128)(2,1)S(1)}, bf16[2,280]{1,0:T(2,128)(2,1)S(1)}, u32[]{:S(2)}, u32[]{:S(2)}) collective-permute-start(bf16[2,280]{1,0:T(2,128)(2,1)S(1)} %concatenate.98), channel_id=1, source_target_pairs={{0,16},{1,17},{2,18},{3,19},{4,20},{5,21},{6,22},{7,23},{8,24},{9,... | collective-permute-start | bytes 3368 | tf_op jit(solution)/shard_map/ppermute | solution.py:408
  6.5 29.0 %collective-permute-start.5 = (bf16[16,1536]{1,0:T(8,128)(2,1)S(1)}, bf16[16,1536]{1,0:T(8,128)(2,1)S(1)}, u32[]{:S(2)}, u32[]{:S(2)}) collective-permute-start(bf16[16,1536]{1,0:T(8,128)(2,1)S(1)} %get-tuple-element.193), channel_id=1, source_target_pairs={{0,16},{1,17},{2,18},{3,19},{4,20},{5,21},{6,22},{7,23},{8,24},{9,... | collective-permute-start | bytes 147464 | tf_op jit(solution)/shard_map/ppermute | solution.py:408
  7.9 21.0 %collective-permute-start.10 = (bf16[16,512]{1,0:T(8,128)(2,1)S(1)}, bf16[16,512]{1,0:T(8,128)(2,1)S(1)}, u32[]{:S(2)}, u32[]{:S(2)}) collective-permute-start(bf16[16,512]{1,0:T(8,128)(2,1)S(1)} %get-tuple-element.209), channel_id=1, source_target_pairs={{0,16},{1,17},{2,18},{3,19},{4,20},{5,21},{6,22},{7,23},{8,24},{9,... | collective-permute-start | bytes 49160 | tf_op jit(solution)/shard_map/ppermute | solution.py:408
  31.9 49.5 %collective-permute-start.11 = (bf16[2,16,512]{2,1,0:T(8,128)(2,1)}, bf16[2,16,512]{2,1,0:T(8,128)(2,1)}, u32[]{:S(2)}, u32[]{:S(2)}) collective-permute-start(bf16[2,16,512]{2,1,0:T(8,128)(2,1)} %pad_maximum_fusion.50), channel_id=1, source_target_pairs={{0,4},{1,5},{2,6},{3,7},{4,0},{5,1},{6,2},{7,3},{8,12},{9,13},{10,... | collective-permute-start | bytes 98312 | tf_op jit(solution)/shard_map/ppermute | solution.py:408
  60.4 21.9 %collective-permute-start.9 = (bf16[2,2,2,2,16,1536]{5,4,0,1,2,3:T(8,128)(2,1)}, bf16[2,2,2,2,16,1536]{5,4,0,1,2,3:T(8,128)(2,1)}, u32[]{:S(2)}, u32[]{:S(2)}) collective-permute-start(bf16[2,2,2,2,16,1536]{5,4,0,1,2,3:T(8,128)(2,1)} %pad_maximum_fusion.16), channel_id=1, source_target_pairs={{0,1},{1,0},{2,3},{3,2},{4,5},{5,4},{6,7},{7,6},{8,9},{9,8},{10,11... | collective-permute-start | bytes 2359304 | tf_op jit(solution)/shard_map/ppermute | solution.py:408
  85.0 20.9 %collective-permute-start.12 = (bf16[2,2,16,512]{3,2,1,0:T(8,128)(2,1)S(1)}, bf16[2,2,16,512]{3,2,1,0:T(8,128)(2,1)S(1)}, u32[]{:S(2)}, u32[]{:S(2)}) collective-permute-start(bf16[2,2,16,512]{3,2,1,0:T(8,128)(2,1)S(1)} %pad_maximum_fusion.46), channel_id=1, source_target_pairs={{0,2},{1,3},{2,0},{3,1},{4,6},{5,7},{6,4},{7,5},{8,10},{9,11},{10,... | collective-permute-start | bytes 196616 | tf_op jit(solution)/shard_map/ppermute | solution.py:408
  105.2 13.4 %collective-permute-start.18 = (bf16[2,2,2,16,2048]{4,3,0,1,2:T(8,128)(2,1)S(1)}, bf16[2,2,2,16,2048]{4,3,0,1,2:T(8,128)(2,1)S(1)}, u32[]{:S(2)}, u32[]{:S(2)}) collective-permute-start(bf16[2,2,2,16,2048]{4,3,0,1,2:T(8,128)(2,1)S(1)} %pad_maximum_fusion.20), channel_id=1, source_target_pairs={{0,2},{1,3},{2,0},{3,1},{4,6},{5,7},{6,4},{7,5},{8,10},{9,11},{10,... | collective-permute-start | bytes 1572872 | tf_op jit(solution)/shard_map/ppermute | solution.py:408
  118.8 21.4 %collective-permute-start.19 = (bf16[2,2,2,2,16,2048]{5,4,0,1,2,3:T(8,128)(2,1)S(1)}, bf16[2,2,2,2,16,2048]{5,4,0,1,2,3:T(8,128)(2,1)S(1)}, u32[]{:S(2)}, u32[]{:S(2)}) collective-permute-start(bf16[2,2,2,2,16,2048]{5,4,0,1,2,3:T(8,128)(2,1)S(1)} %pad_maximum_fusion.12), channel_id=1, source_target_pairs={{0,1},{1,0},{2,3},{3,2},{4,5},{5,4},{6,7},{7,6},{8,9},{9,8},{10,11... | collective-permute-start | bytes 3145736 | tf_op jit(solution)/shard_map/ppermute | solution.py:408
  118.9 38.7 %collective-permute-start.13 = (bf16[2,2,2,16,512]{4,3,2,1,0:T(8,128)(2,1)S(1)}, bf16[2,2,2,16,512]{4,3,2,1,0:T(8,128)(2,1)S(1)}, u32[]{:S(2)}, u32[]{:S(2)}) collective-permute-start(bf16[2,2,2,16,512]{4,3,2,1,0:T(8,128)(2,1)S(1)} %pad_maximum_fusion.38), channel_id=1, source_target_pairs={{0,8},{1,9},{2,10},{3,11},{4,12},{5,13},{6,14},{7,15},{8,0},{9,1},... | collective-permute-start | bytes 393224 | tf_op jit(solution)/shard_map/ppermute | solution.py:408
  119.8 25.2 %collective-permute-start.24 = (bf16[2,2,2,2,64,512]{5,4,3,2,1,0:T(8,128)(2,1)S(1)}, bf16[2,2,2,2,64,512]{5,4,3,2,1,0:T(8,128)(2,1)S(1)}, u32[]{:S(2)}, u32[]{:S(2)}) collective-permute-start(bf16[2,2,2,2,64,512]{5,4,3,2,1,0:T(8,128)(2,1)S(1)} %pad_maximum_fusion.13), channel_id=1, source_target_pairs={{0,1},{1,0},{2,3},{3,2},{4,5},{5,4},{6,7},{7,6},{8,9},{9,8},{10,11... | collective-permute-start | bytes 3145736 | tf_op jit(solution)/shard_map/ppermute | solution.py:408
  161.3 72.5 %collective-permute-start.34 = (bf16[2,2,2,2,16,512]{5,4,3,2,1,0:T(8,128)(2,1)}, bf16[2,2,2,2,16,512]{5,4,3,2,1,0:T(8,128)(2,1)}, u32[]{:S(2)}, u32[]{:S(2)}) collective-permute-start(bf16[2,2,2,2,16,512]{5,4,3,2,1,0:T(8,128)(2,1)} %pad_maximum_fusion.30), channel_id=1, source_target_pairs={{0,1},{1,0},{2,3},{3,2},{4,5},{5,4},{6,7},{7,6},{8,9},{9,8},{10,11... | collective-permute-start | bytes 786440 | tf_op jit(solution)/shard_map/ppermute | solution.py:408
  163.8 50.2 %collective-permute-start.28 = (bf16[2,2,2,16,1536]{4,3,0,1,2:T(8,128)(2,1)}, bf16[2,2,2,16,1536]{4,3,0,1,2:T(8,128)(2,1)}, u32[]{:S(2)}, u32[]{:S(2)}) collective-permute-start(bf16[2,2,2,16,1536]{4,3,0,1,2:T(8,128)(2,1)} %pad_maximum_fusion.26), channel_id=1, source_target_pairs={{0,2},{1,3},{2,0},{3,1},{4,6},{5,7},{6,4},{7,5},{8,10},{9,11},{10,... | collective-permute-start | bytes 1179656 | tf_op jit(solution)/shard_map/ppermute | solution.py:408
  217.4 17.9 %collective-permute-start.29 = (bf16[2,2,2,2,16,1536]{5,4,0,1,2,3:T(8,128)(2,1)}, bf16[2,2,2,2,16,1536]{5,4,0,1,2,3:T(8,128)(2,1)}, u32[]{:S(2)}, u32[]{:S(2)}) collective-permute-start(bf16[2,2,2,2,16,1536]{5,4,0,1,2,3:T(8,128)(2,1)} %pad_maximum_fusion.17), channel_id=1, source_target_pairs={{0,1},{1,0},{2,3},{3,2},{4,5},{5,4},{6,7},{7,6},{8,9},{9,8},{10,11... | collective-permute-start | bytes 2359304 | tf_op jit(solution)/shard_map/ppermute | solution.py:408
  597.4 59.7 %collective-permute-start.55 = (bf16[2,2,2,2,16,1536]{5,4,0,1,2,3:T(8,128)(2,1)S(1)}, bf16[2,2,2,2,16,1536]{5,4,0,1,2,3:T(8,128)(2,1)S(1)}, u32[]{:S(2)}, u32[]{:S(2)}) collective-permute-start(bf16[2,2,2,2,16,1536]{5,4,0,1,2,3:T(8,128)(2,1)S(1)} %bitcast.695), channel_id=1, source_target_pairs={{0,1},{1,0},{2,3},{3,2},{4,5},{5,4},{6,7},{7,6},{8,9},{9,8},{10,11... | collective-permute-start | bytes 2359304 | tf_op jit(solution)/shard_map/ppermute | solution.py:429
  598.9 59.1 %collective-permute-start.50 = (bf16[2,2,2,2,16,1536]{5,4,0,1,2,3:T(8,128)(2,1)S(1)}, bf16[2,2,2,2,16,1536]{5,4,0,1,2,3:T(8,128)(2,1)S(1)}, u32[]{:S(2)}, u32[]{:S(2)}) collective-permute-start(bf16[2,2,2,2,16,1536]{5,4,0,1,2,3:T(8,128)(2,1)S(1)} %bitcast.694), channel_id=1, source_target_pairs={{0,1},{1,0},{2,3},{3,2},{4,5},{5,4},{6,7},{7,6},{8,9},{9,8},{10,11... | collective-permute-start | bytes 2359304 | tf_op jit(solution)/shard_map/ppermute | solution.py:429
  599.8 19.4 %collective-permute-start.65 = (bf16[2,2,2,2,16,512]{5,4,0,1,3,2:T(8,128)(2,1)S(1)}, bf16[2,2,2,2,16,512]{5,4,0,1,3,2:T(8,128)(2,1)S(1)}, u32[]{:S(2)}, u32[]{:S(2)}) collective-permute-start(bf16[2,2,2,2,16,512]{5,4,0,1,3,2:T(8,128)(2,1)S(1)} %bitcast.703), channel_id=1, source_target_pairs={{0,1},{1,0},{2,3},{3,2},{4,5},{5,4},{6,7},{7,6},{8,9},{9,8},{10,11... | collective-permute-start | bytes 786440 | tf_op jit(solution)/shard_map/ppermute | solution.py:429
  600.4 19.4 %collective-permute-start.60 = (bf16[2,2,2,2,16,512]{5,4,0,1,3,2:T(8,128)(2,1)S(1)}, bf16[2,2,2,2,16,512]{5,4,0,1,3,2:T(8,128)(2,1)S(1)}, u32[]{:S(2)}, u32[]{:S(2)}) collective-permute-start(bf16[2,2,2,2,16,512]{5,4,0,1,3,2:T(8,128)(2,1)S(1)} %bitcast.702), channel_id=1, source_target_pairs={{0,1},{1,0},{2,3},{3,2},{4,5},{5,4},{6,7},{7,6},{8,9},{9,8},{10,11... | collective-permute-start | bytes 786440 | tf_op jit(solution)/shard_map/ppermute | solution.py:429
  616.6 42.3 %collective-permute-start.75 = (bf16[2,2,2,2,16,2048]{5,4,0,2,3,1:T(8,128)(2,1)S(1)}, bf16[2,2,2,2,16,2048]{5,4,0,2,3,1:T(8,128)(2,1)S(1)}, u32[]{:S(2)}, u32[]{:S(2)}) collective-permute-start(bf16[2,2,2,2,16,2048]{5,4,0,2,3,1:T(8,128)(2,1)S(1)} %bitcast.693), channel_id=1, source_target_pairs={{0,1},{1,0},{2,3},{3,2},{4,5},{5,4},{6,7},{7,6},{8,9},{9,8},{10,11... | collective-permute-start | bytes 3145736 | tf_op jit(solution)/shard_map/ppermute | solution.py:429
  619.2 41.7 %collective-permute-start.70 = (bf16[2,2,2,2,16,2048]{5,4,0,2,3,1:T(8,128)(2,1)S(1)}, bf16[2,2,2,2,16,2048]{5,4,0,2,3,1:T(8,128)(2,1)S(1)}, u32[]{:S(2)}, u32[]{:S(2)}) collective-permute-start(bf16[2,2,2,2,16,2048]{5,4,0,2,3,1:T(8,128)(2,1)S(1)} %bitcast.692), channel_id=1, source_target_pairs={{0,1},{1,0},{2,3},{3,2},{4,5},{5,4},{6,7},{7,6},{8,9},{9,8},{10,11... | collective-permute-start | bytes 3145736 | tf_op jit(solution)/shard_map/ppermute | solution.py:429
  658.9 19.5 %collective-permute-start.51 = (bf16[2,2,2,16,1536]{4,3,0,1,2:T(8,128)(2,1)S(1)}, bf16[2,2,2,16,1536]{4,3,0,1,2:T(8,128)(2,1)S(1)}, u32[]{:S(2)}, u32[]{:S(2)}) collective-permute-start(bf16[2,2,2,16,1536]{4,3,0,1,2:T(8,128)(2,1)S(1)} %dynamic-slice_bitcast_fusion.5), channel_id=1, source_target_pairs={{0,2},{1,3},{2,0},{3,1},{4,6},{5,7},{6,4},{7,5},{8,10},{9,11},{10,... | collective-permute-start | bytes 1179656 | tf_op jit(solution)/shard_map/ppermute | solution.py:429
  660.9 49.6 %collective-permute-start.76 = (bf16[2,2,2,16,2048]{4,3,0,1,2:T(8,128)(2,1)S(1)}, bf16[2,2,2,16,2048]{4,3,0,1,2:T(8,128)(2,1)S(1)}, u32[]{:S(2)}, u32[]{:S(2)}) collective-permute-start(bf16[2,2,2,16,2048]{4,3,0,1,2:T(8,128)(2,1)S(1)} %dynamic-slice_bitcast_fusion.2), channel_id=1, source_target_pairs={{0,8},{1,9},{2,10},{3,11},{4,12},{5,13},{6,14},{7,15},{8,0},{9,1},... | collective-permute-start | bytes 1572872 | tf_op jit(solution)/shard_map/ppermute | solution.py:429
  661.4 49.5 %collective-permute-start.71 = (bf16[2,2,2,16,2048]{4,3,0,1,2:T(8,128)(2,1)S(1)}, bf16[2,2,2,16,2048]{4,3,0,1,2:T(8,128)(2,1)S(1)}, u32[]{:S(2)}, u32[]{:S(2)}) collective-permute-start(bf16[2,2,2,16,2048]{4,3,0,1,2:T(8,128)(2,1)S(1)} %dynamic-slice_bitcast_fusion.3), channel_id=1, source_target_pairs={{0,8},{1,9},{2,10},{3,11},{4,12},{5,13},{6,14},{7,15},{8,0},{9,1},... | collective-permute-start | bytes 1572872 | tf_op jit(solution)/shard_map/ppermute | solution.py:429
  663.9 49.1 %collective-permute-start.86 = (bf16[2,2,2,64,512]{4,3,0,1,2:T(8,128)(2,1)S(1)}, bf16[2,2,2,64,512]{4,3,0,1,2:T(8,128)(2,1)S(1)}, u32[]{:S(2)}, u32[]{:S(2)}) collective-permute-start(bf16[2,2,2,64,512]{4,3,0,1,2:T(8,128)(2,1)S(1)} %dynamic-slice_bitcast_fusion), channel_id=1, source_target_pairs={{0,2},{1,3},{2,0},{3,1},{4,6},{5,7},{6,4},{7,5},{8,10},{9,11},{10,... | collective-permute-start | bytes 1572872 | tf_op jit(solution)/shard_map/ppermute | solution.py:429
  670.0 43.8 %collective-permute-start.81 = (bf16[2,2,2,64,512]{4,3,0,1,2:T(8,128)(2,1)S(1)}, bf16[2,2,2,64,512]{4,3,0,1,2:T(8,128)(2,1)S(1)}, u32[]{:S(2)}, u32[]{:S(2)}) collective-permute-start(bf16[2,2,2,64,512]{4,3,0,1,2:T(8,128)(2,1)S(1)} %dynamic-slice_bitcast_fusion.1), channel_id=1, source_target_pairs={{0,2},{1,3},{2,0},{3,1},{4,6},{5,7},{6,4},{7,5},{8,10},{9,11},{10,... | collective-permute-start | bytes 1572872 | tf_op jit(solution)/shard_map/ppermute | solution.py:429
  (211 other events, 1445.2 us)

commit v3 on v2

--- a/solution.py
+++ b/solution.py
@@ -345,6 +345,9 @@
     )[1]
     part_mid, grad_gain_two, grad_offset_two = norm_pull(grad_normed_two)
     grad_mid = grad_out + part_mid
+    grad_mid, grad_up_w, grad_down_w = lax.optimization_barrier(
+        (grad_mid, grad_up_w.astype(jnp.bfloat16), grad_down_w.astype(jnp.bfloat16))
+    )
     grad_proj = window_rows(grad_mid, shifted)
     grad_proj_b = jnp.sum(grad_proj, axis=0)
     grad_proj_low = grad_proj.astype(jnp.bfloat16)

time: 747 us -> 778 us (1.041)
  starting transfers between devices: 69.8 us -> 100 us
  waiting for transfers between devices: 173 us -> 143 us
  local copies, waits for them, and re-layouts: 167 us -> 188 us
    ppermute x45, waiting for transfers between devices: 79.2 us -> 63.4 us  [gather_blocks(): other = lax.ppermute(block, 'fsdp', partner_pairs(devices, bit))]
    ppermute x45, starting transfers between devices: 39.6 us -> 55 us  [gather_blocks(): other = lax.ppermute(block, 'fsdp', partner_pairs(devices, bit))]
    ppermute x45, starting transfers between devices: 30.2 us -> 45.4 us  [scatter_sums(): arrived = lax.ppermute(away, 'fsdp', partner_pairs(devices, bit))]
    ppermute x45, waiting for transfers between devices: 94 us -> 80 us  [scatter_sums(): arrived = lax.ppermute(away, 'fsdp', partner_pairs(devices, bit))]
    unnamed x293 -> x353, local copies, waits for them, and re-layouts: 30.5 us -> 34.4 us
    another operation x89 -> x88, other arithmetic: 22.3 us -> 24.9 us  [gather_blocks(): jnp.stack([jnp.where(mine, block, other), jnp.where(mine, other, block)],...]
  transfers between devices with their start and end apart: 90 -> 90, of which waited for: 52 -> 47; matrix products, arithmetic and copies ran while one was open for 19% -> 27% of each run, Pallas kernels for 2% -> 10%
where the time goes in v3:
time: 778 us; the launch traced here: 770 us
  local copies, waits for them, and re-layouts  188 us (24%)
  waiting for transfers between devices  143 us (18%)
  matrix products  132 us (17%)
  Pallas kernels  117 us (15%)
  starting transfers between devices  100 us (13%)
  other arithmetic  84 us (11%)
    pallas_call x2, Pallas kernels, attend_windows_back(): pl.pallas_call(functools.partial(attend_back_kernel, features, mask_add i...  82.2 us
    ppermute x45, waiting for transfers between devices, scatter_sums(): arrived = lax.ppermute(away, 'fsdp', partner_pairs(devices, bit))  80 us
    ppermute x45, waiting for transfers between devices, gather_blocks(): other = lax.ppermute(block, 'fsdp', partner_pairs(devices, bit))  63.4 us
    ppermute x45, starting transfers between devices, gather_blocks(): other = lax.ppermute(block, 'fsdp', partner_pairs(devices, bit))  55 us
    ppermute x45, starting transfers between devices, scatter_sums(): arrived = lax.ppermute(away, 'fsdp', partner_pairs(devices, bit))  45.4 us
    dot_general x2, matrix products, layer_forward(): jnp.dot(normed_two.reshape(-1, features), up_w, preferred_element_type=jn...  43.4 us
    dot_general x8, matrix products, times_transposed(): lax.dot_general(rows_left, rows_right, (((1,), (1,)), ((), ())), preferre...  38.4 us
    pallas_call x2, Pallas kernels, attend_windows(): pl.pallas_call(functools.partial(attend_kernel, features, mask_add is not...  34.8 us
  transfers between devices with their start and end apart: 90, of which 47 were waited for; matrix products, arithmetic and copies ran while one was open for 27% of the time, Pallas kernels for 10%

profile of v3, /device:TPU:0, one launch (start us, length us, event | category | flops | bytes accessed | tf_op | source)
XLA Modules:
  0.0 769.9 jit_solution(4894116295756817287)
XLA Ops:
  68.4 5.7 collective-permute-done.15
  110.4 4.8 collective-permute-done.18
  119.4 17.4 %shard_map.289 = bf16[1280,512]{1,0:T(8,128)(2,1)S(1)} custom-call(bf16[1280,1536]{1,0:T(8,128)(2,1)S(1)} %fusion.14.qkv_ref, f32[1024,64]{1,0:T(8,128)S(1)} %bitcast.644), custom_call_target="tpu_custom_call" | custom-call | flops 671088640 | bytes 5242880 | tf_op jit(solution)/shard_map/pallas_call | solution.py:208
  151.4 7.4 collective-permute-done.25
  158.9 4.8 collective-permute-start.26
  199.3 21.7 %multiply_convert_fusion.1 = (bf16[980,2048]{1,0:T(8,128)(2,1)S(1)}, f32[980,2048]{1,0:T(8,128)}, f32[980,2048]{1,0:T(8,128)}) fusion(f32[2048]{0:T(1024)S(1)} %copy-done.148, bf16[980,512]{1,0:T(8,128)(2,1)S(1)} %copy-done.78, bf16[512,2048]{1,0:T(8,128)(2,1)S(1)} %bitcast.666), kind=kOutput, calls=%fused_computation.23 | convolution fusion | flops 2187673600 | bytes 23179264 | tf_op jit(solution)/shard_map/dot_general | solution.py:281
  238.5 8.8 %collective-permute-done.43 = bf16[2,2,2,64,512]{4,3,2,1,0:T(8,128)(2,1)S(1)} collective-permute-done((bf16[2,2,2,64,512]{4,3,2,1,0:T(8,128)(2,1)S(1)}, bf16[2,2,2,64,512]{4,3,2,1,0:T(8,128)(2,1)S(1)}, u32[]{:S(2)}, u32[]{:S(2)}) %collective-permute-start.43) | collective-permute-done | bytes 524320 | tf_op jit(solution)/shard_map/ppermute | solution.py:411
  284.4 17.4 %shard_map.290 = bf16[1280,512]{1,0:T(8,128)(2,1)S(1)} custom-call(bf16[1280,1536]{1,0:T(8,128)(2,1)S(1)} %fusion.15.qkv_ref, f32[1024,64]{1,0:T(8,128)S(1)} %bitcast.642, f32[4,64,64]{2,1,0:T(8,128)S(1)} %pad.38.refs_0_), custom_call_target="tpu_custom_call" | custom-call | flops 671088640 | bytes 5242880 | tf_op jit(solution)/shard_map/pallas_call | solution.py:208
  333.5 21.7 %multiply_convert_fusion = (bf16[980,2048]{1,0:T(8,128)(2,1)}, f32[980,2048]{1,0:T(8,128)S(1)}, f32[980,2048]{1,0:T(8,128)S(1)}) fusion(f32[2048]{0:T(1024)S(1)} %copy-done.150, bf16[980,512]{1,0:T(8,128)(2,1)} %reshape.611, bf16[512,2048]{1,0:T(8,128)(2,1)} %bitcast.672), kind=kOutput, calls=%fused_computation.10 | convolution fusion | flops 2187673600 | bytes 23179264 | tf_op jit(solution)/shard_map/dot_general | solution.py:281
  355.3 5.6 fusion.140
  366.4 4.7 dot_general.103
  371.2 6.3 convolution_convert_fusion.4
  384.2 6.0 fusion.131
  408.7 41.4 %shard_map.291 = (bf16[1280,1536]{1,0:T(8,128)(2,1)S(1)}, f32[1,1536]{1,0:T(1,128)S(1)}, f32[1024,64]{1,0:T(8,128)S(1)}) custom-call(bf16[1280,1536]{1,0:T(8,128)(2,1)S(1)} %copy-done.3, bf16[1280,512]{1,0:T(8,128)(2,1)S(1)} %convolution_convert_fusion.7.grad_ref, f32[1024,64]{1,0:T(8,128)S(1)} %bitcast.643, f32[4,64,64]{2,1,0:T(8,128)S(1)} %pad.38.refs_0_), custom_call_target="tpu_custom_call" | custom-call | flops 1677721600 | bytes 9175040 | tf_op jit(solution)/shard_map/pallas_call | solution.py:223
  483.6 6.3 convolution_convert_fusion.2
  489.9 9.2 %fusion.141 = (f32[2048]{0:T(1024)}, bf16[980,2048]{1,0:T(8,128)(2,1)S(1)}) fusion(f32[980,2048]{1,0:T(8,128)} %get-tuple-element.98, bf16[980,512]{1,0:T(8,128)(2,1)S(1)} %copy-done.81, bf16[2048,512]{1,0:T(8,128)(2,1)S(1)} %bitcast.669, f32[980,2048]{1,0:T(8,128)} %get-tuple-element.238, f32[2048]{0:T(1024)S(1)} %copy-done.149), kind=kOutput, calls=%fused_computation.541 | convolution fusion | flops 2087319552 | bytes 23187456 | tf_op jit(solution)/shard_map/dot_general | solution.py:79
  504.7 4.6 dot_general.111
  512.5 5.3 fusion.132
  551.9 40.8 %shard_map.292 = (bf16[1280,1536]{1,0:T(8,128)(2,1)S(1)}, f32[1,1536]{1,0:T(1,128)S(1)}, f32[1024,64]{1,0:T(8,128)S(1)}) custom-call(bf16[1280,1536]{1,0:T(8,128)(2,1)S(1)} %copy-done.1, bf16[1280,512]{1,0:T(8,128)(2,1)S(1)} %convolution_convert_fusion.6.grad_ref, f32[1024,64]{1,0:T(8,128)S(1)} %bitcast.645), custom_call_target="tpu_custom_call" | custom-call | flops 1677721600 | bytes 9175040 | tf_op jit(solution)/shard_map/pallas_call | solution.py:223
  603.7 5.4 fusion.143
  701.3 8.0 %collective-permute-done.56 = bf16[2,2,2,16,1536]{4,3,0,1,2:T(8,128)(2,1)S(1)} collective-permute-done((bf16[2,2,2,16,1536]{4,3,0,1,2:T(8,128)(2,1)S(1)}, bf16[2,2,2,16,1536]{4,3,0,1,2:T(8,128)(2,1)S(1)}, u32[]{:S(2)}, u32[]{:S(2)}) %collective-permute-start.56) | collective-permute-done | bytes 393248 | tf_op jit(solution)/shard_map/ppermute | solution.py:432
  720.9 4.2 collective-permute-done.53
  725.5 4.3 collective-permute-done.58
  748.8 5.2 collective-permute-done.87
  (918 shorter events, 497.8 us)
Async XLA Ops:
  2.1 30.7 %collective-permute-start.5 = (bf16[16,1536]{1,0:T(8,128)(2,1)}, bf16[16,1536]{1,0:T(8,128)(2,1)}, u32[]{:S(2)}, u32[]{:S(2)}) collective-permute-start(bf16[16,1536]{1,0:T(8,128)(2,1)} %get-tuple-element.205), channel_id=1, source_target_pairs={{0,16},{1,17},{2,18},{3,19},{4,20},{5,21},{6,22},{7,23},{8,24},{9,... | collective-permute-start | bytes 147464 | tf_op jit(solution)/shard_map/ppermute | solution.py:411
  7.5 22.9 %collective-permute-start.10 = (bf16[16,512]{1,0:T(8,128)(2,1)}, bf16[16,512]{1,0:T(8,128)(2,1)S(1)}, u32[]{:S(2)}, u32[]{:S(2)}) collective-permute-start(bf16[16,512]{1,0:T(8,128)(2,1)} %get-tuple-element.221), channel_id=1, source_target_pairs={{0,16},{1,17},{2,18},{3,19},{4,20},{5,21},{6,22},{7,23},{8,24},{9,... | collective-permute-start | bytes 49160 | tf_op jit(solution)/shard_map/ppermute | solution.py:411
  31.1 65.6 %collective-permute-start.11 = (bf16[2,16,512]{2,1,0:T(8,128)(2,1)}, bf16[2,16,512]{2,1,0:T(8,128)(2,1)}, u32[]{:S(2)}, u32[]{:S(2)}) collective-permute-start(bf16[2,16,512]{2,1,0:T(8,128)(2,1)} %pad_maximum_fusion.50), channel_id=1, source_target_pairs={{0,4},{1,5},{2,6},{3,7},{4,0},{5,1},{6,2},{7,3},{8,12},{9,13},{10,... | collective-permute-start | bytes 98312 | tf_op jit(solution)/shard_map/ppermute | solution.py:411
  74.8 19.2 %collective-permute-start.16 = (bf16[2,16,2048]{2,1,0:T(8,128)(2,1)}, bf16[2,16,2048]{2,1,0:T(8,128)(2,1)}, u32[]{:S(2)}, u32[]{:S(2)}) collective-permute-start(bf16[2,16,2048]{2,1,0:T(8,128)(2,1)} %pad_maximum_fusion.39), channel_id=1, source_target_pairs={{0,8},{1,9},{2,10},{3,11},{4,12},{5,13},{6,14},{7,15},{8,0},{9,1},... | collective-permute-start | bytes 393224 | tf_op jit(solution)/shard_map/ppermute | solution.py:411
  106.5 61.6 %collective-permute-start.13 = (bf16[2,2,2,16,512]{4,3,2,1,0:T(8,128)(2,1)S(1)}, bf16[2,2,2,16,512]{4,3,2,1,0:T(8,128)(2,1)S(1)}, u32[]{:S(2)}, u32[]{:S(2)}) collective-permute-start(bf16[2,2,2,16,512]{4,3,2,1,0:T(8,128)(2,1)S(1)} %pad_maximum_fusion.38), channel_id=1, source_target_pairs={{0,8},{1,9},{2,10},{3,11},{4,12},{5,13},{6,14},{7,15},{8,0},{9,1},... | collective-permute-start | bytes 393224 | tf_op jit(solution)/shard_map/ppermute | solution.py:411
  115.4 23.0 %collective-permute-start.19 = (bf16[2,2,2,2,16,2048]{5,4,0,1,2,3:T(8,128)(2,1)S(1)}, bf16[2,2,2,2,16,2048]{5,4,0,1,2,3:T(8,128)(2,1)S(1)}, u32[]{:S(2)}, u32[]{:S(2)}) collective-permute-start(bf16[2,2,2,2,16,2048]{5,4,0,1,2,3:T(8,128)(2,1)S(1)} %pad_maximum_fusion.12), channel_id=1, source_target_pairs={{0,1},{1,0},{2,3},{3,2},{4,5},{5,4},{6,7},{7,6},{8,9},{9,8},{10,11... | collective-permute-start | bytes 3145736 | tf_op jit(solution)/shard_map/ppermute | solution.py:411
  115.5 21.2 %collective-permute-start.21 = (bf16[2,64,512]{2,1,0:T(8,128)(2,1)S(1)}, bf16[2,64,512]{2,1,0:T(8,128)(2,1)S(1)}, u32[]{:S(2)}, u32[]{:S(2)}) collective-permute-start(bf16[2,64,512]{2,1,0:T(8,128)(2,1)S(1)} %pad_maximum_fusion.40), channel_id=1, source_target_pairs={{0,4},{1,5},{2,6},{3,7},{4,0},{5,1},{6,2},{7,3},{8,12},{9,13},{10,... | collective-permute-start | bytes 393224 | tf_op jit(solution)/shard_map/ppermute | solution.py:411
  146.9 91.6 %collective-permute-start.23 = (bf16[2,2,2,64,512]{4,3,2,1,0:T(8,128)(2,1)}, bf16[2,2,2,64,512]{4,3,2,1,0:T(8,128)(2,1)}, u32[]{:S(2)}, u32[]{:S(2)}) collective-permute-start(bf16[2,2,2,64,512]{4,3,2,1,0:T(8,128)(2,1)} %pad_maximum_fusion.21), channel_id=1, source_target_pairs={{0,8},{1,9},{2,10},{3,11},{4,12},{5,13},{6,14},{7,15},{8,0},{9,1},... | collective-permute-start | bytes 1572872 | tf_op jit(solution)/shard_map/ppermute | solution.py:411
  169.7 79.0 %collective-permute-start.34 = (bf16[2,2,2,2,16,512]{5,4,3,2,1,0:T(8,128)(2,1)}, bf16[2,2,2,2,16,512]{5,4,3,2,1,0:T(8,128)(2,1)}, u32[]{:S(2)}, u32[]{:S(2)}) collective-permute-start(bf16[2,2,2,2,16,512]{5,4,3,2,1,0:T(8,128)(2,1)} %pad_maximum_fusion.30), channel_id=1, source_target_pairs={{0,1},{1,0},{2,3},{3,2},{4,5},{5,4},{6,7},{7,6},{8,9},{9,8},{10,11... | collective-permute-start | bytes 786440 | tf_op jit(solution)/shard_map/ppermute | solution.py:411
  173.0 17.4 %collective-permute-start.28 = (bf16[2,2,2,16,1536]{4,3,0,1,2:T(8,128)(2,1)}, bf16[2,2,2,16,1536]{4,3,0,1,2:T(8,128)(2,1)}, u32[]{:S(2)}, u32[]{:S(2)}) collective-permute-start(bf16[2,2,2,16,1536]{4,3,0,1,2:T(8,128)(2,1)} %pad_maximum_fusion.26), channel_id=1, source_target_pairs={{0,2},{1,3},{2,0},{3,1},{4,6},{5,7},{6,4},{7,5},{8,10},{9,11},{10,... | collective-permute-start | bytes 1179656 | tf_op jit(solution)/shard_map/ppermute | solution.py:411
  198.1 24.7 %collective-permute-start.40 = (bf16[64,512]{1,0:T(8,128)(2,1)S(1)}, bf16[64,512]{1,0:T(8,128)(2,1)S(1)}, u32[]{:S(2)}, u32[]{:S(2)}) collective-permute-start(bf16[64,512]{1,0:T(8,128)(2,1)S(1)} %copy-done.91), channel_id=1, source_target_pairs={{0,16},{1,17},{2,18},{3,19},{4,20},{5,21},{6,22},{7,23},{8,24},{9,... | collective-permute-start | bytes 196616 | tf_op jit(solution)/shard_map/ppermute | solution.py:411
  237.9 14.9 %collective-permute-start.38 = (bf16[2,2,2,16,2048]{4,3,0,1,2:T(8,128)(2,1)S(1)}, bf16[2,2,2,16,2048]{4,3,0,1,2:T(8,128)(2,1)S(1)}, u32[]{:S(2)}, u32[]{:S(2)}) collective-permute-start(bf16[2,2,2,16,2048]{4,3,0,1,2:T(8,128)(2,1)S(1)} %pad_maximum_fusion.23), channel_id=1, source_target_pairs={{0,2},{1,3},{2,0},{3,1},{4,6},{5,7},{6,4},{7,5},{8,10},{9,11},{10,... | collective-permute-start | bytes 1572872 | tf_op jit(solution)/shard_map/ppermute | solution.py:411
  252.8 63.1 %collective-permute-start.44 = (bf16[2,2,2,2,64,512]{5,4,3,2,1,0:T(8,128)(2,1)}, bf16[2,2,2,2,64,512]{5,4,3,2,1,0:T(8,128)(2,1)}, u32[]{:S(2)}, u32[]{:S(2)}) collective-permute-start(bf16[2,2,2,2,64,512]{5,4,3,2,1,0:T(8,128)(2,1)} %pad_maximum_fusion.15), channel_id=1, source_target_pairs={{0,1},{1,0},{2,3},{3,2},{4,5},{5,4},{6,7},{7,6},{8,9},{9,8},{10,11... | collective-permute-start | bytes 3145736 | tf_op jit(solution)/shard_map/ppermute | solution.py:411
  254.7 65.5 %collective-permute-start.39 = (bf16[2,2,2,2,16,2048]{5,4,0,1,2,3:T(8,128)(2,1)}, bf16[2,2,2,2,16,2048]{5,4,0,1,2,3:T(8,128)(2,1)}, u32[]{:S(2)}, u32[]{:S(2)}) collective-permute-start(bf16[2,2,2,2,16,2048]{5,4,0,1,2,3:T(8,128)(2,1)} %pad_maximum_fusion.14), channel_id=1, source_target_pairs={{0,1},{1,0},{2,3},{3,2},{4,5},{5,4},{6,7},{7,6},{8,9},{9,8},{10,11... | collective-permute-start | bytes 3145736 | tf_op jit(solution)/shard_map/ppermute | solution.py:411
  543.6 146.1 %collective-permute-start.80 = (bf16[2,2,2,2,64,512]{5,4,0,1,2,3:T(8,128)(2,1)}, bf16[2,2,2,2,64,512]{5,4,0,1,2,3:T(8,128)(2,1)}, u32[]{:S(2)}, u32[]{:S(2)}) collective-permute-start(bf16[2,2,2,2,64,512]{5,4,0,1,2,3:T(8,128)(2,1)} %bitcast.632), channel_id=1, source_target_pairs={{0,1},{1,0},{2,3},{3,2},{4,5},{5,4},{6,7},{7,6},{8,9},{9,8},{10,11... | collective-permute-start | bytes 3145736 | tf_op jit(solution)/shard_map/ppermute | solution.py:432
  546.8 146.2 %collective-permute-start.85 = (bf16[2,2,2,2,64,512]{5,4,0,1,2,3:T(8,128)(2,1)}, bf16[2,2,2,2,64,512]{5,4,0,1,2,3:T(8,128)(2,1)}, u32[]{:S(2)}, u32[]{:S(2)}) collective-permute-start(bf16[2,2,2,2,64,512]{5,4,0,1,2,3:T(8,128)(2,1)} %bitcast.631), channel_id=1, source_target_pairs={{0,1},{1,0},{2,3},{3,2},{4,5},{5,4},{6,7},{7,6},{8,9},{9,8},{10,11... | collective-permute-start | bytes 3145736 | tf_op jit(solution)/shard_map/ppermute | solution.py:432
  550.0 145.3 %collective-permute-start.70 = (bf16[2,2,2,2,16,2048]{5,4,0,2,3,1:T(8,128)(2,1)}, bf16[2,2,2,2,16,2048]{5,4,0,2,3,1:T(8,128)(2,1)}, u32[]{:S(2)}, u32[]{:S(2)}) collective-permute-start(bf16[2,2,2,2,16,2048]{5,4,0,2,3,1:T(8,128)(2,1)} %bitcast.634), channel_id=1, source_target_pairs={{0,1},{1,0},{2,3},{3,2},{4,5},{5,4},{6,7},{7,6},{8,9},{9,8},{10,11... | collective-permute-start | bytes 3145736 | tf_op jit(solution)/shard_map/ppermute | solution.py:432
  551.4 96.8 %collective-permute-start.60 = (bf16[2,2,2,2,16,512]{5,4,0,1,3,2:T(8,128)(2,1)}, bf16[2,2,2,2,16,512]{5,4,0,1,3,2:T(8,128)(2,1)}, u32[]{:S(2)}, u32[]{:S(2)}) collective-permute-start(bf16[2,2,2,2,16,512]{5,4,0,1,3,2:T(8,128)(2,1)} %bitcast.638), channel_id=1, source_target_pairs={{0,1},{1,0},{2,3},{3,2},{4,5},{5,4},{6,7},{7,6},{8,9},{9,8},{10,11... | collective-permute-start | bytes 786440 | tf_op jit(solution)/shard_map/ppermute | solution.py:432
  648.3 38.9 %collective-permute-start.50 = (bf16[2,2,2,2,16,1536]{5,4,0,1,2,3:T(8,128)(2,1)S(1)}, bf16[2,2,2,2,16,1536]{5,4,0,1,2,3:T(8,128)(2,1)S(1)}, u32[]{:S(2)}, u32[]{:S(2)}) collective-permute-start(bf16[2,2,2,2,16,1536]{5,4,0,1,2,3:T(8,128)(2,1)S(1)} %bitcast.692), channel_id=1, source_target_pairs={{0,1},{1,0},{2,3},{3,2},{4,5},{5,4},{6,7},{7,6},{8,9},{9,8},{10,11... | collective-permute-start | bytes 2359304 | tf_op jit(solution)/shard_map/ppermute | solution.py:432
  689.7 19.6 %collective-permute-start.56 = (bf16[2,2,2,16,1536]{4,3,0,1,2:T(8,128)(2,1)S(1)}, bf16[2,2,2,16,1536]{4,3,0,1,2:T(8,128)(2,1)S(1)}, u32[]{:S(2)}, u32[]{:S(2)}) collective-permute-start(bf16[2,2,2,16,1536]{4,3,0,1,2:T(8,128)(2,1)S(1)} %dynamic-slice_bitcast_fusion.4), channel_id=1, source_target_pairs={{0,2},{1,3},{2,0},{3,1},{4,6},{5,7},{6,4},{7,5},{8,10},{9,11},{10,... | collective-permute-start | bytes 1179656 | tf_op jit(solution)/shard_map/ppermute | solution.py:432
  693.0 48.8 %collective-permute-start.81 = (bf16[2,2,2,64,512]{4,3,0,1,2:T(8,128)(2,1)S(1)}, bf16[2,2,2,64,512]{4,3,0,1,2:T(8,128)(2,1)S(1)}, u32[]{:S(2)}, u32[]{:S(2)}) collective-permute-start(bf16[2,2,2,64,512]{4,3,0,1,2:T(8,128)(2,1)S(1)} %dynamic-slice_bitcast_fusion.1), channel_id=1, source_target_pairs={{0,2},{1,3},{2,0},{3,1},{4,6},{5,7},{6,4},{7,5},{8,10},{9,11},{10,... | collective-permute-start | bytes 1572872 | tf_op jit(solution)/shard_map/ppermute | solution.py:432
  695.2 48.3 %collective-permute-start.86 = (bf16[2,2,2,64,512]{4,3,0,1,2:T(8,128)(2,1)S(1)}, bf16[2,2,2,64,512]{4,3,0,1,2:T(8,128)(2,1)S(1)}, u32[]{:S(2)}, u32[]{:S(2)}) collective-permute-start(bf16[2,2,2,64,512]{4,3,0,1,2:T(8,128)(2,1)S(1)} %dynamic-slice_bitcast_fusion), channel_id=1, source_target_pairs={{0,2},{1,3},{2,0},{3,1},{4,6},{5,7},{6,4},{7,5},{8,10},{9,11},{10,... | collective-permute-start | bytes 1572872 | tf_op jit(solution)/shard_map/ppermute | solution.py:432
  698.5 45.8 %collective-permute-start.71 = (bf16[2,2,2,16,2048]{4,3,0,1,2:T(8,128)(2,1)S(1)}, bf16[2,2,2,16,2048]{4,3,0,1,2:T(8,128)(2,1)S(1)}, u32[]{:S(2)}, u32[]{:S(2)}) collective-permute-start(bf16[2,2,2,16,2048]{4,3,0,1,2:T(8,128)(2,1)S(1)} %dynamic-slice_bitcast_fusion.3), channel_id=1, source_target_pairs={{0,8},{1,9},{2,10},{3,11},{4,12},{5,13},{6,14},{7,15},{8,0},{9,1},... | collective-permute-start | bytes 1572872 | tf_op jit(solution)/shard_map/ppermute | solution.py:432
  700.8 44.3 %collective-permute-start.76 = (bf16[2,2,2,16,2048]{4,3,0,1,2:T(8,128)(2,1)S(1)}, bf16[2,2,2,16,2048]{4,3,0,1,2:T(8,128)(2,1)S(1)}, u32[]{:S(2)}, u32[]{:S(2)}) collective-permute-start(bf16[2,2,2,16,2048]{4,3,0,1,2:T(8,128)(2,1)S(1)} %dynamic-slice_bitcast_fusion.2), channel_id=1, source_target_pairs={{0,8},{1,9},{2,10},{3,11},{4,12},{5,13},{6,14},{7,15},{8,0},{9,1},... | collective-permute-start | bytes 1572872 | tf_op jit(solution)/shard_map/ppermute | solution.py:432
  (241 other events, 1515.6 us)
